TPU v7x, 32 devices: a whole 2x2x4 slice. The times are simulated.
32 devices in a mesh: head: 4 (over x, core), blk: 8 (over z, y).
Axes of the slice: x: 2, y: 2, z: 4, core: 2. Of those that a mesh axis runs over, the one named last changes fastest.
Arguments:
- query: bfloat16 [4096, 8192], P(('blk', 'head'))
- key: bfloat16 [4096, 1024], P(('blk', 'head'))
- value: bfloat16 [4096, 1024], P(('blk', 'head')), may hold values from -6 to 6
- output_gradient: bfloat16 [4096, 8192], P(('blk', 'head')), may hold values from -6 to 6
- pair_codes: int32 [8, 8, 8], P('blk'), may hold values from 0 to 15
- pair_counts: int32 [8, 8], P('blk'), may hold values from 1 to 8
Outputs:
- attn_out: bfloat16 [4096, 8192], P(('blk', 'head'))
- grad_query: bfloat16 [4096, 8192], P(('blk', 'head'))
- key_gradient: bfloat16 [4096, 1024], P(('blk', 'head'))
- value_gradient: bfloat16 [4096, 1024], P(('blk', 'head'))
All inputs are finite; a program needn't handle non-finite values.
Results may differ from a plain program's by a relative error of at most 0.015.
Values may be sent and summed in bfloat16 or wider, within the bound.
A program may use at most 128 MiB of HBM per device.

v0:
```python
import functools
import math

import jax
import jax.numpy as jnp
from jax import lax
from jax.experimental import pallas as pl
from jax.experimental.pallas import tpu as pltpu
from jax.sharding import PartitionSpec as P

QUERY_HEADS = 64
KEY_VALUE_HEADS = 8
HEAD_SIZE = 128
BLOCK = 128
NEGATIVE_FILL = -1e30

NT = (((1,), (1,)), ((), ()))
NN = (((1,), (0,)), ((), ()))
TN = (((0,), (0,)), ((), ()))
MESH = pl.DeviceIdType.MESH
LINE = 2


def dot(a, b, dims):
    return lax.dot_general(a, b, dims, preferred_element_type=jnp.float32)


def query_block(nblocks, base_ref, turn):
    return lax.rem(base_ref[1] + base_ref[2] * turn, nblocks)


def attend(
    nstep, nblocks, heads, split, base_ref, codes_ref, counts_ref,
    q_ref, g_ref, k_ref, v_ref, out_ref, dkv_ref,
    lst, cnt, qs, gs, scores, out_t, dq_t, dk, dv,
):
    def place_of(base, s):
        at = lax.rem(base - s + nstep, nstep)
        if not split:
            return at
        far = lax.rem(at + base, LINE)
        return at // LINE + far * (nstep // LINE)

    scale = HEAD_SIZE ** (-0.5)
    c2 = scale * math.log2(math.e)
    turn = pl.program_id(0)
    qb = query_block(nblocks, base_ref, turn)
    width = heads * BLOCK

    @pl.when(turn == 0)
    def _():
        dk[...] = jnp.zeros_like(dk)
        dv[...] = jnp.zeros_like(dv)
        base = base_ref[0]
        for b in range(nblocks):
            cnt[b] = 1
            lst[b * nstep * nblocks] = place_of(base, 0) * nblocks + b

        def over_steps(s, _):
            place = place_of(base, s) * nblocks

            def over_codes(i, _):
                code = codes_ref[s, i]
                row = code // nblocks
                col = code - row * nblocks

                @pl.when(jnp.logical_or(s != 0, row != col))
                def _():
                    n = cnt[row]
                    lst[row * nstep * nblocks + n] = place + col
                    cnt[row] = n + 1

                return 0

            return lax.fori_loop(0, counts_ref[s], over_codes, 0)

        lax.fori_loop(0, nstep, over_steps, 0)

    n = cnt[qb]
    first = qb * nstep * nblocks

    def rows_of(i):
        return pl.ds(pl.multiple_of(lst[first + i] * BLOCK, BLOCK), BLOCK)

    for h in range(heads):
        cols = slice(h * BLOCK, (h + 1) * BLOCK)
        qs[cols, :] = q_ref[:, cols]
        gs[cols, :] = g_ref[:, cols]

    key_at = lax.broadcasted_iota(jnp.int32, (BLOCK, width), 0)
    query_at = lax.broadcasted_iota(jnp.int32, (BLOCK, width), 1) % BLOCK
    s0 = dot(k_ref[rows_of(0), :], qs[...], NT)
    s0 = jnp.where(key_at <= query_at, s0, NEGATIVE_FILL)
    scores[0] = s0
    top = jnp.max(s0, axis=0, keepdims=True)

    def score_pass(i, top):
        s = dot(k_ref[rows_of(i), :], qs[...], NT)
        scores[i] = s
        return jnp.maximum(top, jnp.max(s, axis=0, keepdims=True))

    top = lax.fori_loop(1, n, score_pass, top)
    out_t[...] = jnp.zeros_like(out_t)

    def weight_pass(i, total):
        w = jnp.exp2((scores[i] - top) * c2)
        scores[i] = w
        out_t[...] += dot(v_ref[rows_of(i), :], w.astype(jnp.bfloat16), TN)
        return total + jnp.sum(w, axis=0, keepdims=True)

    total = lax.fori_loop(0, n, weight_pass, jnp.zeros((1, width), jnp.float32))
    inv = 1.0 / total

    row_dots = []
    for h in range(heads):
        cols = slice(h * BLOCK, (h + 1) * BLOCK)
        attn = jnp.transpose(out_t[:, cols] * inv[:, cols]).astype(jnp.bfloat16)
        out_ref[:, cols] = attn
        prod = attn.astype(jnp.float32) * g_ref[:, cols].astype(jnp.float32)
        row_dots.append(jnp.sum(jnp.transpose(prod), axis=0, keepdims=True))
    row_dot = jnp.concatenate(row_dots, axis=1)
    dq_t[...] = jnp.zeros_like(dq_t)

    def grad_pass(i, _):
        rows = rows_of(i)
        p = scores[i] * inv
        dv[rows, :] += dot(p.astype(jnp.bfloat16), gs[...], NN)
        dp = dot(v_ref[rows, :], gs[...], NT)
        ds = (p * (dp - row_dot)).astype(jnp.bfloat16)
        dk[rows, :] += dot(ds, qs[...], NN)
        dq_t[...] += dot(k_ref[rows, :], ds, TN)
        return 0

    lax.fori_loop(0, n, grad_pass, 0)
    for h in range(heads):
        cols = slice(h * BLOCK, (h + 1) * BLOCK)
        out_ref[:, width + h * BLOCK : width + (h + 1) * BLOCK] = jnp.transpose(
            dq_t[:, cols] * scale
        ).astype(jnp.bfloat16)

    @pl.when(turn == nblocks - 1)
    def _():
        dkv_ref[:, :HEAD_SIZE] = (dk[...] * scale).astype(jnp.bfloat16)
        dkv_ref[:, HEAD_SIZE:] = dv[...].astype(jnp.bfloat16)


def attention(split, base, codes, counts, q, g, kv):
    nstep = codes.shape[0]
    rows = q.shape[0]
    width = HEAD_SIZE * (QUERY_HEADS // KEY_VALUE_HEADS)
    gcol = g.shape[1] // width - 1
    heads = width // HEAD_SIZE
    nblocks = rows // BLOCK
    keys = kv.shape[0]
    f32, bf16 = jnp.float32, jnp.bfloat16
    flops = 6 * 2 * 30 * width * BLOCK * HEAD_SIZE
    return pl.pallas_call(
        functools.partial(attend, nstep, nblocks, heads, split),
        out_shape=(
            jax.ShapeDtypeStruct((rows, 2 * width), bf16),
            jax.ShapeDtypeStruct((keys, 2 * HEAD_SIZE), bf16),
        ),
        grid_spec=pltpu.PrefetchScalarGridSpec(
            num_scalar_prefetch=3,
            grid=(nblocks,),
            in_specs=[
                pl.BlockSpec((BLOCK, width), lambda i, *_: (i, 0)),
                pl.BlockSpec((BLOCK, width), lambda i, *_: (i, gcol)),
                pl.BlockSpec((keys, HEAD_SIZE), lambda i, *_: (0, 0)),
                pl.BlockSpec((keys, HEAD_SIZE), lambda i, *_: (0, 1)),
            ],
            out_specs=[
                pl.BlockSpec(
                    (BLOCK, 2 * width),
                    lambda i, base, *_: (query_block(nblocks, base, i), 0),
                ),
                pl.BlockSpec((keys, 2 * HEAD_SIZE), lambda i, *_: (0, 0)),
            ],
            scratch_shapes=[
                pltpu.SMEM((nblocks * nstep * nblocks,), jnp.int32),
                pltpu.SMEM((nblocks,), jnp.int32),
                pltpu.VMEM((width, HEAD_SIZE), bf16),
                pltpu.VMEM((width, HEAD_SIZE), bf16),
                pltpu.VMEM((nstep * nblocks, BLOCK, width), f32),
                pltpu.VMEM((HEAD_SIZE, width), f32),
                pltpu.VMEM((HEAD_SIZE, width), f32),
                pltpu.VMEM((keys, HEAD_SIZE), f32),
                pltpu.VMEM((keys, HEAD_SIZE), f32),
            ],
        ),
        compiler_params=pltpu.CompilerParams(vmem_limit_bytes=44 * 2**20),
        cost_estimate=pl.CostEstimate(
            flops=16 * flops, bytes_accessed=2**23, transcendentals=30 * width * BLOCK
        ),
    )(base, codes, counts, q, g, kv, kv)


def greet(nh, nblk, whole, me, blk):
    barrier = pltpu.get_barrier_semaphore()
    for m in range(1, nh):
        pl.semaphore_signal(
            barrier, inc=1, device_id=(lax.rem(me + m, nh), blk), device_id_type=MESH
        )
    others = nblk if whole else 1
    for m in range(1, others):
        pl.semaphore_signal(
            barrier, inc=1, device_id=(me, lax.rem(blk + m, nblk)), device_id_type=MESH
        )
    pl.semaphore_wait(barrier, nh - 1 + others - 1)


def aligned(index, size):
    return pl.ds(pl.multiple_of(index * size, size), size)


def remote(src, dst, sems, device):
    return pltpu.make_async_remote_copy(
        src_ref=src, dst_ref=dst, send_sem=sems[0], recv_sem=sems[1],
        device_id=device, device_id_type=MESH,
    )


def enter(
    nh, nblk, whole, q, k, v, g, q0, g0, kv0, kv1,
    send, recv, local, up_s, up_r, down_s, down_r, y_s, y_r,
):
    me, blk = lax.axis_index("head"), lax.axis_index("blk")
    greet(nh, nblk, whole, me, blk)
    rows = q.shape[0]
    qc = q0.shape[1]
    group = nh * rows
    nz = nblk // LINE
    hi, lo = blk // LINE, lax.rem(blk, LINE)
    keys = (kv0, kv1)

    def parts(n):
        if n < 4:
            j, which = n // 2, n % 2
            at = aligned((hi * nh if whole else 0) + me, rows)
            dst = keys[j].at[at, pl.ds(which * HEAD_SIZE, HEAD_SIZE)]
            return (k, v)[which], HEAD_SIZE, j, dst
        return (q, g)[n - 4], qc, 0, (q0, g0)[n - 4].at[aligned(me, rows), :]

    def to_peer(n, m):
        src, cols, j, dst = parts(n)
        peer = lax.rem(me + m, nh)
        return remote(
            src.at[:, aligned(peer * 2 + j, cols)], dst,
            (send.at[n, m - 1], recv.at[n, m - 1]), (peer, blk),
        )

    def own(n):
        src, cols, j, dst = parts(n)
        return pltpu.make_async_copy(src.at[:, aligned(me * 2 + j, cols)], dst, local.at[n])

    order = (2, 3, 1) if nh == 4 else tuple(range(1, nh))

    def start(n):
        for m in order:
            to_peer(n, m).start()
        own(n).start()

    def arrived(n):
        for m in order:
            to_peer(n, m).wait_recv()
        own(n).wait()

    def block(j, z):
        return keys[j].at[aligned(z, group), :]

    def up(j, d):
        return remote(
            block(j, hi - d), block(j, hi - d), (up_s.at[j, d], up_r.at[j, d]),
            (me, blk + LINE),
        )

    def down(j, d):
        return remote(
            block(j, hi + d), block(j, hi + d), (down_s.at[j, d], down_r.at[j, d]),
            (me, blk - LINE),
        )

    def across(z, slot):
        return remote(
            block(0, z), block(0, nz + z), (y_s.at[slot], y_r.at[slot]),
            (me, blk + 1 - 2 * lo),
        )

    def pass_on(j, d):
        if d > 0:
            pl.when(hi - d >= 0)(lambda: up(j, d - 1).wait_recv())
        if d < nz - 1:
            pl.when(jnp.logical_and(hi - d >= 0, hi < nz - 1))(lambda: up(j, d).start())
        if d > 0:
            pl.when(hi + d < nz)(lambda: down(j, d - 1).wait_recv())
        if d < nz - 1:
            pl.when(jnp.logical_and(hi + d < nz, hi > 0))(lambda: down(j, d).start())
        if j > 0:
            return
        if d == 0:
            across(hi, 0).start()
        else:
            pl.when(hi - d >= 0)(lambda: across(hi - d, d).start())
            pl.when(hi + d < nz)(lambda: across(hi + d, nz - 1 + d).start())

    for n in range(4):
        start(n)
    for j in range(2):
        arrived(2 * j)
        arrived(2 * j + 1)
        if whole:
            pass_on(j, 0)
    start(4)
    start(5)
    if whole:
        for d in range(1, nz):
            pass_on(0, d)
            pass_on(1, d)
        across(hi, 0).wait()
        for d in range(1, nz):
            pl.when(hi - d >= 0)(lambda d=d: across(hi - d, d).wait())
            pl.when(hi + d < nz)(lambda d=d: across(hi + d, nz - 1 + d).wait())
        for j in range(2):
            for d in range(nz - 1):
                pl.when(jnp.logical_and(hi - d >= 0, hi < nz - 1))(
                    lambda j=j, d=d: up(j, d).wait_send()
                )
                pl.when(jnp.logical_and(hi + d < nz, hi > 0))(
                    lambda j=j, d=d: down(j, d).wait_send()
                )
    arrived(4)
    arrived(5)
    for n in range(6):
        for m in order:
            to_peer(n, m).wait_send()


def leave(
    nh, nblk, whole, o0, r1, r2, r3, o1, d0, y0, d1, attn, dq, dk, dv,
    y_in, up_in, down_in, sums, home, send, recv, local, near,
    up_s, up_r, down_s, down_r, y_s, y_r,
):
    me, blk = lax.axis_index("head"), lax.axis_index("blk")
    greet(nh, nblk, whole, me, blk)
    grads = (d0, d1)
    rows = attn.shape[0]
    group = nh * rows
    half = o1.shape[1] // 2
    kw = dk.shape[1] // nh
    f32, bf16 = jnp.float32, jnp.bfloat16
    nz = nblk // LINE
    hi, lo = blk // LINE, lax.rem(blk, LINE)

    def part(n, row):
        if n < 2:
            return (
                o1.at[aligned(row, rows), pl.ds(n * half, half)],
                (attn, dq)[n].at[:, aligned(me * 2 + 1, half)],
            )
        return (
            home.at[aligned(row, rows), pl.ds((n - 2) * kw, kw)],
            (dk, dv)[n - 2].at[:, aligned(me, kw)],
        )

    def to_peer(n, m):
        peer = lax.rem(me + m, nh)
        src, dst = part(n, peer)
        return remote(src, dst, (send.at[n, m - 1], recv.at[n, m - 1]), (peer, blk))

    def own(n):
        src, dst = part(n, me)
        return pltpu.make_async_copy(src, dst, local.at[n])

    def brought(m, which):
        cols = pl.ds(which * half, half)
        src = o0.at[aligned(me, rows), cols] if m == 0 else (r1, r2, r3)[m - 1].at[:, cols]
        dst = (attn, dq)[which].at[:, aligned(lax.rem(me - m + nh, nh) * 2, half)]
        return pltpu.make_async_copy(src, dst, near.at[m, which])

    order = (2, 3, 1) if nh == 4 else tuple(range(1, nh))

    def across(z):
        return remote(
            d1.at[aligned(nz + z, group), :], y_in.at[z], (y_s.at[z], y_r.at[z]),
            (me, blk + 1 - 2 * lo),
        )

    def start_outs():
        for n in range(2):
            for m in order:
                to_peer(n, m).start()
            own(n).start()
        for m in range(nh):
            for which in range(2):
                brought(m, which).start()

    def up(z):
        return remote(sums.at[z], up_in.at[z], (up_s.at[z], up_r.at[z]), (me, blk + LINE))

    def down(z):
        return remote(
            sums.at[z], down_in.at[z], (down_s.at[z], down_r.at[z]), (me, blk - LINE)
        )

    def keep(z, value):
        for j in range(2):
            sums[z, j] = value[j].astype(bf16)

    def mine(z):
        at = pl.ds(z * group, group)
        return [
            d0[at, :].astype(f32) + y0[at, :].astype(f32),
            d1[at, :].astype(f32) + y_in[z].astype(f32),
        ]

    def with_in(value, arrived, z):
        return [value[j] + arrived[z, j].astype(f32) for j in range(2)]

    def finish(value):
        for j in range(2):
            for which in range(2):
                at = which * 2 + j
                home[:, at * HEAD_SIZE : (at + 1) * HEAD_SIZE] = value[j][
                    :, which * HEAD_SIZE : (which + 1) * HEAD_SIZE
                ].astype(bf16)

    if whole:
        far_first = sorted(range(nz), key=lambda z: -abs(2 * z - nz + 1))
        for z in far_first:
            across(z).start()
        start_outs()
        for z in far_first:
            across(z).wait_recv()

            @pl.when(hi < z)
            def _(z=z):
                @pl.when(hi == 0)
                def _():
                    keep(z, mine(z))

                @pl.when(hi > 0)
                def _():
                    up(z).wait_recv()
                    keep(z, with_in(mine(z), up_in, z))

                up(z).start()

            @pl.when(hi > z)
            def _(z=z):
                @pl.when(hi == nz - 1)
                def _():
                    keep(z, mine(z))

                @pl.when(hi < nz - 1)
                def _():
                    down(z).wait_recv()
                    keep(z, with_in(mine(z), down_in, z))

                down(z).start()

        for z in range(nz):
            @pl.when(hi == z)
            def _(z=z):
                value = mine(z)
                if z > 0:
                    up(z).wait_recv()
                    value = with_in(value, up_in, z)
                if z < nz - 1:
                    down(z).wait_recv()
                    value = with_in(value, down_in, z)
                finish(value)

    else:
        start_outs()
        finish([grads[j][...].astype(f32) for j in range(2)])
    for n in (2, 3):
        for m in order:
            to_peer(n, m).start()
        own(n).start()
    if whole:
        for z in range(nz):
            across(z).wait_send()
            pl.when(hi < z)(lambda z=z: up(z).wait_send())
            pl.when(hi > z)(lambda z=z: down(z).wait_send())
    for n in range(4):
        for m in order:
            to_peer(n, m).wait()
        own(n).wait()
    for m in range(nh):
        for which in range(2):
            brought(m, which).wait()


def permuted(block, axis, distance):
    size = lax.axis_size(axis)
    return lax.ppermute(block, axis, [(i, (i + distance) % size) for i in range(size)])


def swapped(block):
    return lax.ppermute(block, "blk", [(i, i ^ 1) for i in range(lax.axis_size("blk"))])


def body(query, key, value, output_gradient, pair_codes, pair_counts):
    rows = query.shape[0]
    nh = lax.axis_size("head")
    nblk = lax.axis_size("blk")
    codes, counts = pair_codes[0], pair_counts[0]
    nstep = codes.shape[0]
    whole = nblk == nstep
    nz = nblk // LINE
    group = nh * rows
    bf16 = jnp.bfloat16
    dma = pltpu.SemaphoreType.DMA
    anywhere = pl.BlockSpec(memory_space=pl.ANY)
    in_vmem = pl.BlockSpec(memory_space=pltpu.VMEM)
    width = query.shape[1] // KEY_VALUE_HEADS
    pair = 2 * HEAD_SIZE
    like = jax.ShapeDtypeStruct
    q0, g0, kv0, kv1 = pl.pallas_call(
        functools.partial(enter, nh, nblk, whole),
        out_shape=(
            like((group, width), bf16),
            like((group, width), bf16),
            like((group * (nblk if whole else 1), pair), bf16),
            like((group * (nz if whole else 1), pair), bf16),
        ),
        in_specs=[anywhere] * 4,
        out_specs=[anywhere] * 4,
        scratch_shapes=[
            dma((6, nh - 1)), dma((6, nh - 1)), dma((6,)),
            dma((2, nz)), dma((2, nz)), dma((2, nz)), dma((2, nz)),
            dma((2 * nz,)), dma((2 * nz,)),
        ],
        compiler_params=pltpu.CompilerParams(collective_id=0, has_side_effects=True),
    )(query, key, value, output_gradient)
    query, output_gradient, q0, g0, kv0, kv1 = lax.optimization_barrier(
        (query, output_gradient, q0, g0, kv0, kv1)
    )
    me = lax.axis_index("head")

    def second(m):
        at = (lax.rem(me + m, nh) * 2 + 1) * width
        return jnp.concatenate(
            [
                lax.dynamic_slice_in_dim(x, at, width, 1)
                for x in (query, output_gradient)
            ],
            axis=1,
        )

    if whole:
        kv1 = jnp.concatenate([kv1, swapped(kv1)], axis=0)
    else:
        kv0, kv1 = (
            jnp.concatenate(
                [kv] + [permuted(kv, "blk", nstep - i) for i in range(1, nstep)], axis=0
            )
            for kv in (kv0, kv1)
        )
    qg1 = jnp.concatenate(
        [second(0)] + [permuted(second(m), "head", m) for m in range(1, nh)], axis=0
    )
    start = lax.axis_index("blk") if whole else jnp.int32(0)
    base0 = jnp.stack([start, jnp.int32(0), jnp.int32(1)]).astype(jnp.int32)
    base1 = jnp.stack([start, me, jnp.int32(nh - 1)]).astype(jnp.int32)

    def returned(grad):
        if whole:
            return grad
        parts = grad.reshape(nstep, group, -1)
        total = parts[0].astype(jnp.float32)
        for i in range(1, nstep):
            total += permuted(parts[i], "blk", i - nstep).astype(jnp.float32)
        return total.astype(bf16)

    o0, d0 = attention(whole, base0, codes, counts, q0, g0, kv0)
    came = [
        permuted(
            lax.dynamic_slice_in_dim(o0, lax.rem(me + m, nh) * rows, rows, 0), "head", m
        )
        for m in range(1, nh)
    ]
    y0 = swapped(d0[nz * group :]) if whole else d0
    d0 = returned(d0)
    o1, d1 = attention(whole, base1, codes, counts, qg1, qg1, kv1)
    d1 = returned(d1)
    y0 = y0 if whole else d0
    y_slots = (nz if whole else 1, group, pair)
    slots = (nz if whole else 1, 2, group, pair)
    return pl.pallas_call(
        functools.partial(leave, nh, nblk, whole),
        out_shape=(
            like(query.shape, bf16), like(query.shape, bf16),
            like(key.shape, bf16), like(value.shape, bf16),
        ),
        in_specs=[anywhere] * 5 + [in_vmem] * 3,
        out_specs=[anywhere] * 4,
        scratch_shapes=[
            pltpu.VMEM(y_slots, bf16), pltpu.VMEM(slots, bf16), pltpu.VMEM(slots, bf16),
            pltpu.VMEM(slots, bf16), pltpu.VMEM((group, 2 * pair), bf16),
            dma((4, nh - 1)), dma((4, nh - 1)), dma((4,)), dma((nh, 2)),
            dma((nz,)), dma((nz,)), dma((nz,)), dma((nz,)),
            dma((nz,)), dma((nz,)),
        ],
        compiler_params=pltpu.CompilerParams(
            collective_id=1, has_side_effects=True, vmem_limit_bytes=40 * 2**20
        ),
    )(o0, *came, o1, d0, y0, d1)


def solution(mesh):
    tokens = P(("blk", "head"), None)
    return jax.shard_map(
        body,
        mesh=mesh,
        in_specs=(tokens,) * 4 + (P("blk", None, None), P("blk", None)),
        out_specs=(tokens,) * 4,
        check_vma=False,
    )
```

profile of v0, /device:TPU:9, one launch (start us, length us, event | category | flops | bytes accessed | tf_op | source)
XLA Modules:
  0.0 208.8 jit_solution(17109693321591229783)
XLA Ops:
  0.6 0.0 copy-start.8
  0.6 45.4 %shard_map.93 = (bf16[512,1024]{1,0:T(8,128)(2,1)}, bf16[512,1024]{1,0:T(8,128)(2,1)}, bf16[4096,256]{1,0:T(8,128)(2,1)}, bf16[2048,256]{1,0:T(8,128)(2,1)}) custom-call(bf16[128,8192]{1,0:T(8,128)(2,1)} %q.1, bf16[128,1024]{1,0:T(8,128)(2,1)} %k.1, bf16[128,1024]{1,0:T(8,128)(2,1)} %v.1, bf16[128,8192]{1,0:T(8,128)(2,1)} %g.1), custom_call_target="tpu_custom_call" | custom-call | tf_op jit(solution)/shard_map/pallas_call | solution.py:519
  46.0 0.4 collective-permute-start.6
  46.4 0.0 copy-done.8
  46.4 2.1 %constant_dynamic-slice_fusion.6 = (bf16[128,1024]{1,0:T(8,128)(2,1)S(1)}, bf16[128,1024]{1,0:T(8,128)(2,1)S(1)}, bf16[128,1024]{1,0:T(8,128)(2,1)S(1)}, bf16[12...) fusion(bf16[128,8192]{1,0:T(8,128)(2,1)} %g.1, ...), kind=kLoop, calls=%fused_computation.11 | loop fusion | bytes 4194320 | tf_op jit(solution)/shard_map/dynamic_slice | solution.py:545
  48.5 0.9 pad_maximum_fusion.2
  49.4 0.7 collective-permute-start.3
  50.0 0.9 pad_maximum_fusion.3
  50.9 1.2 collective-permute-start.4
  52.2 0.8 pad_maximum_fusion.4
  53.0 0.0 collective-permute-start.5
  53.0 0.1 pad_add_fusion.base_ref
  53.1 0.0 copy-done.4
  53.1 0.0 copy-done.6
  53.1 0.0 copy-done.7
  53.1 0.0 copy-start.3
  53.1 1.6 copy-done.3
  54.7 1.2 copy-done.5
  55.9 33.6 %shard_map.94 = (bf16[512,2048]{1,0:T(8,128)(2,1)S(1)}, bf16[4096,256]{1,0:T(8,128)(2,1)S(1)}) custom-call(s32[3]{0:T(128)S(1)} %pad_add_fusion.base_ref, s32[8,8]{1,0:T(8,128)S(1)} %bitcast.4, s32[8]{0:T(128)S(1)} %bitcast.6, bf16[512,1024]{1,0:T(8,128)(2,1)S(1)} %copy-done.4, bf16[512,1024]{1,0:T(8,128)(2,1)S(1)} %copy-done.5, ...), custom_call_target="tpu_custom_call" | custom-call | flops 96636764160 | bytes 8388608 | tf_op jit(solution)/shard_map/pallas_call | solution.py:157
  89.5 1.1 slice.3
  90.6 1.3 copy-done
  91.9 0.0 collective-permute-start.7
  91.9 0.1 pad_add_fusion.1.base_ref
  92.0 0.1 constant_dynamic-slice_fusion.8
  92.1 0.0 collective-permute-done.3
  92.1 0.7 collective-permute-start.2
  92.8 0.0 collective-permute-done.4
  92.8 1.2 collective-permute-start.1
  94.0 0.0 collective-permute-done.5
  94.1 0.6 collective-permute-start
  94.6 0.0 copy-done.10
  94.6 3.1 %pad_maximum_fusion.q_ref.g_ref = bf16[512,2048]{1,0:T(8,128)(2,1)S(1)} fusion(bf16[128,2048]{1,0:T(8,128)(2,1)} %collective-permute-done.5, bf16[128,2048]{1,0:T(8,128)(2,1)} %collective-permute-done.4, bf16[128,2048]{1,0:T(8,128)(2,1)} %collective-permute-done.3, bf16[128,1024]{1,0:T(8,128)(2,1)S(1)} %get-tuple-element.36, bf16[128,1024]{1,0:T(8,128)(2,1)S(1)} %copy-done.10), kind=kLoop, calls=%fused_computation | loop fusion | flops 10485760 | bytes 4194304 | tf_op jit(solution)/shard_map/concatenate | solution.py:560
  97.8 0.0 collective-permute-done.6
  97.8 0.0 copy-done.9
  97.8 1.4 pad_maximum_fusion.1.k_ref.v_ref
  99.1 0.0 copy-start.1
  99.2 33.9 %shard_map.95 = (bf16[512,2048]{1,0:T(8,128)(2,1)S(1)}, bf16[4096,256]{1,0:T(8,128)(2,1)S(1)}) custom-call(s32[3]{0:T(128)S(1)} %pad_add_fusion.1.base_ref, s32[8,8]{1,0:T(8,128)S(1)} %bitcast.5, s32[8]{0:T(128)S(1)} %bitcast.7, bf16[512,2048]{1,0:T(8,128)(2,1)S(1)} %pad_maximum_fusion.q_ref.g_ref, bf16[512,2048]{1,0:T(8,128)(2,1)S(1)} %pad_maximum_fusion.q_ref.g_ref, ...), custom_call_target="tpu_custom_call" | custom-call | flops 96636764160 | bytes 8388608 | tf_op jit(solution)/shard_map/pallas_call | solution.py:157
  133.0 0.0 copy-start.2
  133.0 1.3 copy-done.2
  134.3 0.0 collective-permute-done.2.r3
  134.3 0.0 collective-permute-done.1.r2
  134.3 0.0 collective-permute-done.r1
  134.3 0.0 collective-permute-done.7.y0
  134.4 70.4 %shard_map.96 = (bf16[128,8192]{1,0:T(8,128)(2,1)S(1)}, bf16[128,8192]{1,0:T(8,128)(2,1)S(1)}, bf16[128,1024]{1,0:T(8,128)(2,1)S(1)}, bf16[128,1024]{1,0:T(8,128)(2,1)S(1)}) custom-call(bf16[512,2048]{1,0:T(8,128)(2,1)S(1)} %get-tuple-element.25.o0, bf16[128,2048]{1,0:T(8,128)(2,1)S(1)} %collective-permute-done.r1, ...), custom_call_target="tpu_custom_call" | custom-call | tf_op jit(solution)/shard_map/pallas_call | solution.py:590
  204.8 1.3 copy.14
  206.1 1.3 copy.15
  207.4 0.7 copy.16
  208.1 0.7 copy.17
  (8 shorter events, 0.0 us)
Async XLA Ops:
  0.6 45.8 %copy-start.8 = (bf16[128,8192]{1,0:T(8,128)(2,1)S(1)}, bf16[128,8192]{1,0:T(8,128)(2,1)}, u32[]{:S(2)}) copy-start(bf16[128,8192]{1,0:T(8,128)(2,1)} %q.1) | copy-start | bytes 6291460
  46.0 51.7 %collective-permute-start.6 = (bf16[2048,256]{1,0:T(8,128)(2,1)}, bf16[2048,256]{1,0:T(8,128)(2,1)}, u32[]{:S(2)}, u32[]{:S(2)}) collective-permute-start(bf16[2048,256]{1,0:T(8,128)(2,1)} %get-tuple-element.28), channel_id=1, source_target_pairs={{0,1},{1,0},{2,3},{3,2},{4,5},{5,4},{6,7},{7,6},{8,9},{9,8},{10,11... | collective-permute-start | bytes 3145736 | tf_op jit(solution)/shard_map/ppermute | solution.py:500
  48.5 4.6 %copy-start.4 = (bf16[512,1024]{1,0:T(8,128)(2,1)S(1)}, bf16[512,1024]{1,0:T(8,128)(2,1)}, u32[]{:S(2)}) copy-start(bf16[512,1024]{1,0:T(8,128)(2,1)} %get-tuple-element.22.q_ref) | copy-start | bytes 3145732
  48.5 4.6 %copy-start.6 = (s32[1,8,8]{2,1,0:T(8,128)S(1)}, s32[1,8,8]{2,1,0:T(8,128)}, u32[]{:S(2)}) copy-start(s32[1,8,8]{2,1,0:T(8,128)} %param.10) | copy-start | bytes 772
  48.5 4.6 %copy-start.7 = (s32[1,8]{1,0:T(1,128)S(1)}, s32[1,8]{1,0:T(1,128)}, u32[]{:S(2)}) copy-start(s32[1,8]{1,0:T(1,128)} %param.11) | copy-start | bytes 100
  49.4 42.8 %collective-permute-start.3 = (bf16[128,2048]{1,0:T(8,128)(2,1)}, bf16[128,2048]{1,0:T(8,128)(2,1)}, u32[]{:S(2)}, u32[]{:S(2)}) collective-permute-start(bf16[128,2048]{1,0:T(8,128)(2,1)} %pad_maximum_fusion.2), channel_id=1, source_target_pairs={{0,8},{8,16},{16,24},{24,0},{1,9},{9,17},{17,25},{25,1},{2,10},{10... | collective-permute-start | bytes 1572872 | tf_op jit(solution)/shard_map/ppermute | solution.py:496
  50.9 41.9 %collective-permute-start.4 = (bf16[128,2048]{1,0:T(8,128)(2,1)}, bf16[128,2048]{1,0:T(8,128)(2,1)}, u32[]{:S(2)}, u32[]{:S(2)}) collective-permute-start(bf16[128,2048]{1,0:T(8,128)(2,1)} %pad_maximum_fusion.3), channel_id=1, source_target_pairs={{0,16},{8,24},{16,0},{24,8},{1,17},{9,25},{17,1},{25,9},{2,18},{10... | collective-permute-start | bytes 1572872 | tf_op jit(solution)/shard_map/ppermute | solution.py:496
  53.0 41.1 %collective-permute-start.5 = (bf16[128,2048]{1,0:T(8,128)(2,1)}, bf16[128,2048]{1,0:T(8,128)(2,1)}, u32[]{:S(2)}, u32[]{:S(2)}) collective-permute-start(bf16[128,2048]{1,0:T(8,128)(2,1)} %pad_maximum_fusion.4), channel_id=1, source_target_pairs={{0,24},{8,0},{16,8},{24,16},{1,25},{9,1},{17,9},{25,17},{2,26},{10... | collective-permute-start | bytes 1572872 | tf_op jit(solution)/shard_map/ppermute | solution.py:496
  53.1 1.6 copy-start.3
  54.7 1.2 copy-start.5
  90.6 1.3 copy-start
  91.9 42.4 %collective-permute-start.7 = (bf16[2048,256]{1,0:T(8,128)(2,1)}, bf16[2048,256]{1,0:T(8,128)(2,1)S(1)}, u32[]{:S(2)}, u32[]{:S(2)}) collective-permute-start(bf16[2048,256]{1,0:T(8,128)(2,1)} %slice.3), channel_id=1, source_target_pairs={{0,1},{1,0},{2,3},{3,2},{4,5},{5,4},{6,7},{7,6},{8,9},{9,8},{10,11... | collective-permute-start | bytes 3145736 | tf_op jit(solution)/shard_map/ppermute | solution.py:500
  91.9 2.7 %copy-start.10 = (bf16[128,1024]{1,0:T(8,128)(2,1)S(1)}, bf16[128,1024]{1,0:T(8,128)(2,1)}, u32[]{:S(2)}) copy-start(bf16[128,1024]{1,0:T(8,128)(2,1)} %get-tuple-element.46) | copy-start | bytes 786436
  92.1 42.2 %collective-permute-start.2 = (bf16[128,2048]{1,0:T(8,128)(2,1)S(1)}, bf16[128,2048]{1,0:T(8,128)(2,1)S(1)}, u32[]{:S(2)}, u32[]{:S(2)}) collective-permute-start(bf16[128,2048]{1,0:T(8,128)(2,1)S(1)} %get-tuple-element.40), channel_id=1, source_target_pairs={{0,24},{8,0},{16,8},{24,16},{1,25},{9,1},{17,9},{25,17},{2,26},{10... | collective-permute-start | bytes 1572872 | tf_op jit(solution)/shard_map/ppermute | solution.py:496
  92.8 41.5 %collective-permute-start.1 = (bf16[128,2048]{1,0:T(8,128)(2,1)S(1)}, bf16[128,2048]{1,0:T(8,128)(2,1)S(1)}, u32[]{:S(2)}, u32[]{:S(2)}) collective-permute-start(bf16[128,2048]{1,0:T(8,128)(2,1)S(1)} %get-tuple-element.41), channel_id=1, source_target_pairs={{0,16},{8,24},{16,0},{24,8},{1,17},{9,25},{17,1},{25,9},{2,18},{10... | collective-permute-start | bytes 1572872 | tf_op jit(solution)/shard_map/ppermute | solution.py:496
  94.1 40.3 %collective-permute-start = (bf16[128,2048]{1,0:T(8,128)(2,1)S(1)}, bf16[128,2048]{1,0:T(8,128)(2,1)S(1)}, u32[]{:S(2)}, u32[]{:S(2)}) collective-permute-start(bf16[128,2048]{1,0:T(8,128)(2,1)S(1)} %get-tuple-element.42), channel_id=1, source_target_pairs={{0,8},{8,16},{16,24},{24,0},{1,9},{9,17},{17,25},{25,1},{2,10},{10... | collective-permute-start | bytes 1572872 | tf_op jit(solution)/shard_map/ppermute | solution.py:496
  94.6 3.2 %copy-start.9 = (bf16[2048,256]{1,0:T(8,128)(2,1)S(1)}, bf16[2048,256]{1,0:T(8,128)(2,1)}, u32[]{:S(2)}) copy-start(bf16[2048,256]{1,0:T(8,128)(2,1)} %get-tuple-element.28) | copy-start | bytes 3145732
  99.1 35.2 %copy-start.1 = (bf16[4096,256]{1,0:T(8,128)(2,1)S(1)}, bf16[4096,256]{1,0:T(8,128)(2,1)}, u32[]{:S(2)}) copy-start(bf16[4096,256]{1,0:T(8,128)(2,1)} %copy-done) | copy-start | bytes 6291460
  133.0 1.3 copy-start.2
where the time goes:
time: 211 us; the launch traced here: 209 us
  Pallas kernels  183 us (87%)
  local copies, waits for them, and re-layouts  12.8 us (6%)
  other arithmetic  7.25 us (3%)
  starting transfers between devices  4.74 us (2%)
    pallas_call x1, Pallas kernels, body(): pl.pallas_call(functools.partial(leave, nh, nblk, whole), out_shape=(like...  70.4 us
    pallas_call x2, Pallas kernels, attention(): pl.pallas_call(functools.partial(attend, nstep, nblocks, heads, split), o...  67.5 us
    pallas_call x1, Pallas kernels, body(): pl.pallas_call(functools.partial(enter, nh, nblk, whole), out_shape=(like...  45.4 us
    unnamed x26, local copies, waits for them, and re-layouts  9.51 us
    ppermute x6, starting transfers between devices, permuted(): lax.ppermute(block, axis, [(i, (i + distance) % size) for i in range(size)])  4.38 us
  transfers between devices with their start and end apart: 8, of which 0 were waited for; matrix products, arithmetic and copies ran while one was open for 5% of the time, Pallas kernels for 32%

commit v1 on v0

--- a/solution.py
+++ b/solution.py
@@ -30,10 +30,13 @@
 
 
 def attend(
-    nstep, nblocks, heads, split, base_ref, codes_ref, counts_ref,
-    q_ref, g_ref, k_ref, v_ref, out_ref, dkv_ref,
-    lst, cnt, qs, gs, scores, out_t, dq_t, dk, dv,
+    nstep, nblocks, heads, split, inputs, base_ref, codes_ref, counts_ref, *refs
 ):
+    asked, (k_ref, v_ref, out_ref) = refs[:inputs], refs[inputs : inputs + 3]
+    shares = 2 if split else 1
+    dkv_refs = refs[inputs + 3 : inputs + 3 + shares]
+    lst, cnt, qs, gs, scores, out_t, dq_t, dk, dv = refs[inputs + 3 + shares :]
+
     def place_of(base, s):
         at = lax.rem(base - s + nstep, nstep)
         if not split:
@@ -46,6 +49,9 @@
     turn = pl.program_id(0)
     qb = query_block(nblocks, base_ref, turn)
     width = heads * BLOCK
+    room = nstep * nblocks
+    both = 2 * BLOCK
+    f32, bf16 = jnp.float32, jnp.bfloat16
 
     @pl.when(turn == 0)
     def _():
@@ -54,7 +60,7 @@
         base = base_ref[0]
         for b in range(nblocks):
             cnt[b] = 1
-            lst[b * nstep * nblocks] = place_of(base, 0) * nblocks + b
+            lst[b * room] = place_of(base, 0) * nblocks + b
 
         def over_steps(s, _):
             place = place_of(base, s) * nblocks
@@ -67,7 +73,7 @@
                 @pl.when(jnp.logical_or(s != 0, row != col))
                 def _():
                     n = cnt[row]
-                    lst[row * nstep * nblocks + n] = place + col
+                    lst[row * room + n] = place + col
                     cnt[row] = n + 1
 
                 return 0
@@ -77,96 +83,147 @@
         lax.fori_loop(0, nstep, over_steps, 0)
 
     n = cnt[qb]
-    first = qb * nstep * nblocks
+    first = qb * room
+    chunks = (n + 1) // 2
 
     def rows_of(i):
-        return pl.ds(pl.multiple_of(lst[first + i] * BLOCK, BLOCK), BLOCK)
-
-    for h in range(heads):
-        cols = slice(h * BLOCK, (h + 1) * BLOCK)
-        qs[cols, :] = q_ref[:, cols]
-        gs[cols, :] = g_ref[:, cols]
-
-    key_at = lax.broadcasted_iota(jnp.int32, (BLOCK, width), 0)
-    query_at = lax.broadcasted_iota(jnp.int32, (BLOCK, width), 1) % BLOCK
-    s0 = dot(k_ref[rows_of(0), :], qs[...], NT)
-    s0 = jnp.where(key_at <= query_at, s0, NEGATIVE_FILL)
-    scores[0] = s0
-    top = jnp.max(s0, axis=0, keepdims=True)
-
-    def score_pass(i, top):
-        s = dot(k_ref[rows_of(i), :], qs[...], NT)
-        scores[i] = s
+        at = lst[first + jnp.where(i < n, i, 0)]
+        return pl.ds(pl.multiple_of(at * BLOCK, BLOCK), BLOCK)
+
+    def two(ref, c):
+        return jnp.concatenate([ref[rows_of(2 * c), :], ref[rows_of(2 * c + 1), :]], axis=0)
+
+    def turned(x):
+        return jnp.transpose(x.astype(f32)).astype(bf16)
+
+    def load(q_ref, g_ref, g_at):
+        for h in range(heads):
+            cols = slice(h * BLOCK, (h + 1) * BLOCK)
+            qs[cols, :] = q_ref[:, cols]
+            gs[cols, :] = g_ref[:, g_at + h * BLOCK : g_at + (h + 1) * BLOCK]
+
+    if inputs == 2:
+        load(asked[0], asked[1], 0)
+    else:
+        for m in range(inputs):
+            pl.when(turn == m)(functools.partial(load, asked[m], asked[m], width))
+
+    tiles = [slice(t * both, (t + 1) * both) for t in range(width // both)]
+
+    def tile_top(s, cols, c, top):
+        scores[c, :, cols] = s
         return jnp.maximum(top, jnp.max(s, axis=0, keepdims=True))
 
-    top = lax.fori_loop(1, n, score_pass, top)
+    def ending(s, c):
+        last = jnp.where(2 * c + 1 < n, s[BLOCK:], NEGATIVE_FILL)
+        return jnp.concatenate([s[:BLOCK], last], axis=0)
+
+    key_at = lax.broadcasted_iota(jnp.int32, (both, both), 0)
+    query_at = lax.broadcasted_iota(jnp.int32, (both, both), 1) % BLOCK
+    seen = jnp.logical_or(key_at <= query_at, key_at >= BLOCK)
+    kk = two(k_ref, 0)
+    tops = []
+    for cols in tiles:
+        s = jnp.where(seen, dot(kk, qs[cols, :], NT), NEGATIVE_FILL)
+        tops.append(tile_top(ending(s, 0), cols, 0, jnp.full((1, both), NEGATIVE_FILL, f32)))
+
+    def score_pass(c, tops):
+        kk = two(k_ref, c)
+        return tuple(
+            tile_top(ending(dot(kk, qs[cols, :], NT), c), cols, c, top)
+            for cols, top in zip(tiles, tops)
+        )
+
+    tops = lax.fori_loop(1, chunks, score_pass, tuple(tops))
     out_t[...] = jnp.zeros_like(out_t)
 
-    def weight_pass(i, total):
-        w = jnp.exp2((scores[i] - top) * c2)
-        scores[i] = w
-        out_t[...] += dot(v_ref[rows_of(i), :], w.astype(jnp.bfloat16), TN)
-        return total + jnp.sum(w, axis=0, keepdims=True)
-
-    total = lax.fori_loop(0, n, weight_pass, jnp.zeros((1, width), jnp.float32))
-    inv = 1.0 / total
+    def weight_pass(c, totals):
+        vt = turned(two(v_ref, c))
+        new = []
+        for cols, top, total in zip(tiles, tops, totals):
+            w = jnp.exp2((scores[c, :, cols] - top) * c2)
+            scores[c, :, cols] = w
+            out_t[:, cols] += dot(vt, w.astype(bf16), NN)
+            new.append(total + jnp.sum(w, axis=0, keepdims=True))
+        return tuple(new)
+
+    zero = tuple(jnp.zeros((1, both), f32) for _ in tiles)
+    totals = lax.fori_loop(0, chunks, weight_pass, zero)
+    invs = [1.0 / total for total in totals]
 
     row_dots = []
     for h in range(heads):
         cols = slice(h * BLOCK, (h + 1) * BLOCK)
-        attn = jnp.transpose(out_t[:, cols] * inv[:, cols]).astype(jnp.bfloat16)
+        inv = invs[h // 2][:, (h % 2) * BLOCK : (h % 2 + 1) * BLOCK]
+        attn = jnp.transpose(out_t[:, cols] * inv).astype(bf16)
         out_ref[:, cols] = attn
-        prod = attn.astype(jnp.float32) * g_ref[:, cols].astype(jnp.float32)
+        prod = attn.astype(f32) * gs[cols, :].astype(f32)
         row_dots.append(jnp.sum(jnp.transpose(prod), axis=0, keepdims=True))
-    row_dot = jnp.concatenate(row_dots, axis=1)
+    row_dots = [
+        jnp.concatenate(row_dots[2 * t : 2 * t + 2], axis=1) for t in range(len(tiles))
+    ]
     dq_t[...] = jnp.zeros_like(dq_t)
 
-    def grad_pass(i, _):
-        rows = rows_of(i)
-        p = scores[i] * inv
-        dv[rows, :] += dot(p.astype(jnp.bfloat16), gs[...], NN)
-        dp = dot(v_ref[rows, :], gs[...], NT)
-        ds = (p * (dp - row_dot)).astype(jnp.bfloat16)
-        dk[rows, :] += dot(ds, qs[...], NN)
-        dq_t[...] += dot(k_ref[rows, :], ds, TN)
+    def grad_pass(c, _):
+        kt = turned(two(k_ref, c))
+        vv = two(v_ref, c)
+        dv_now = jnp.zeros((both, HEAD_SIZE), f32)
+        dk_now = jnp.zeros((both, HEAD_SIZE), f32)
+        for cols, inv, row_dot in zip(tiles, invs, row_dots):
+            p = scores[c, :, cols] * inv
+            dv_now += dot(p.astype(bf16), gs[cols, :], NN)
+            dp = dot(vv, gs[cols, :], NT)
+            ds = (p * (dp - row_dot)).astype(bf16)
+            dk_now += dot(ds, qs[cols, :], NN)
+            dq_t[:, cols] += dot(kt, ds, NN)
+        for i in range(2):
+            rows = rows_of(2 * c + i)
+            part = slice(i * BLOCK, (i + 1) * BLOCK)
+            dv[rows, :] += dv_now[part]
+            dk[rows, :] += dk_now[part]
         return 0
 
-    lax.fori_loop(0, n, grad_pass, 0)
+    lax.fori_loop(0, chunks, grad_pass, 0)
     for h in range(heads):
         cols = slice(h * BLOCK, (h + 1) * BLOCK)
         out_ref[:, width + h * BLOCK : width + (h + 1) * BLOCK] = jnp.transpose(
             dq_t[:, cols] * scale
-        ).astype(jnp.bfloat16)
+        ).astype(bf16)
 
     @pl.when(turn == nblocks - 1)
     def _():
-        dkv_ref[:, :HEAD_SIZE] = (dk[...] * scale).astype(jnp.bfloat16)
-        dkv_ref[:, HEAD_SIZE:] = dv[...].astype(jnp.bfloat16)
-
-
-def attention(split, base, codes, counts, q, g, kv):
+        for share, ref in enumerate(dkv_refs):
+            rows = slice(share * ref.shape[0], (share + 1) * ref.shape[0])
+            ref[:, :HEAD_SIZE] = (dk[rows, :] * scale).astype(bf16)
+            ref[:, HEAD_SIZE:] = dv[rows, :].astype(bf16)
+
+
+def attention(split, base, codes, counts, asked, kv):
     nstep = codes.shape[0]
-    rows = q.shape[0]
+    inputs = len(asked)
     width = HEAD_SIZE * (QUERY_HEADS // KEY_VALUE_HEADS)
-    gcol = g.shape[1] // width - 1
     heads = width // HEAD_SIZE
+    rows = asked[0].shape[0] * (1 if inputs == 2 else inputs)
     nblocks = rows // BLOCK
     keys = kv.shape[0]
+    shares = 2 if split else 1
     f32, bf16 = jnp.float32, jnp.bfloat16
     flops = 6 * 2 * 30 * width * BLOCK * HEAD_SIZE
+    whole_block = lambda i, *_: (0, 0)
+    if inputs == 2:
+        q_specs = [pl.BlockSpec((BLOCK, width), lambda i, *_: (i, 0))] * 2
+    else:
+        q_specs = [pl.BlockSpec((BLOCK, 2 * width), whole_block)] * inputs
     return pl.pallas_call(
-        functools.partial(attend, nstep, nblocks, heads, split),
-        out_shape=(
-            jax.ShapeDtypeStruct((rows, 2 * width), bf16),
-            jax.ShapeDtypeStruct((keys, 2 * HEAD_SIZE), bf16),
-        ),
+        functools.partial(attend, nstep, nblocks, heads, split, inputs),
+        out_shape=[jax.ShapeDtypeStruct((rows, 2 * width), bf16)]
+        + [jax.ShapeDtypeStruct((keys // shares, 2 * HEAD_SIZE), bf16)] * shares,
         grid_spec=pltpu.PrefetchScalarGridSpec(
             num_scalar_prefetch=3,
             grid=(nblocks,),
-            in_specs=[
-                pl.BlockSpec((BLOCK, width), lambda i, *_: (i, 0)),
-                pl.BlockSpec((BLOCK, width), lambda i, *_: (i, gcol)),
-                pl.BlockSpec((keys, HEAD_SIZE), lambda i, *_: (0, 0)),
+            in_specs=q_specs
+            + [
+                pl.BlockSpec((keys, HEAD_SIZE), whole_block),
                 pl.BlockSpec((keys, HEAD_SIZE), lambda i, *_: (0, 1)),
             ],
             out_specs=[
@@ -174,25 +231,25 @@
                     (BLOCK, 2 * width),
                     lambda i, base, *_: (query_block(nblocks, base, i), 0),
                 ),
-                pl.BlockSpec((keys, 2 * HEAD_SIZE), lambda i, *_: (0, 0)),
-            ],
+            ]
+            + [pl.BlockSpec((keys // shares, 2 * HEAD_SIZE), whole_block)] * shares,
             scratch_shapes=[
                 pltpu.SMEM((nblocks * nstep * nblocks,), jnp.int32),
                 pltpu.SMEM((nblocks,), jnp.int32),
                 pltpu.VMEM((width, HEAD_SIZE), bf16),
                 pltpu.VMEM((width, HEAD_SIZE), bf16),
-                pltpu.VMEM((nstep * nblocks, BLOCK, width), f32),
+                pltpu.VMEM((nstep * nblocks // 2, 2 * BLOCK, width), f32),
                 pltpu.VMEM((HEAD_SIZE, width), f32),
                 pltpu.VMEM((HEAD_SIZE, width), f32),
                 pltpu.VMEM((keys, HEAD_SIZE), f32),
                 pltpu.VMEM((keys, HEAD_SIZE), f32),
             ],
         ),
-        compiler_params=pltpu.CompilerParams(vmem_limit_bytes=44 * 2**20),
+        compiler_params=pltpu.CompilerParams(vmem_limit_bytes=48 * 2**20),
         cost_estimate=pl.CostEstimate(
             flops=16 * flops, bytes_accessed=2**23, transcendentals=30 * width * BLOCK
         ),
-    )(base, codes, counts, q, g, kv, kv)
+    )(base, codes, counts, *asked, kv, kv)
 
 
 def greet(nh, nblk, whole, me, blk):
@@ -221,9 +278,10 @@
 
 
 def enter(
-    nh, nblk, whole, q, k, v, g, q0, g0, kv0, kv1,
-    send, recv, local, up_s, up_r, down_s, down_r, y_s, y_r,
+    nh, nblk, whole, q, k, v, g, q0, g0, kv0, kv1, *refs
 ):
+    cuts = refs[:nh]
+    send, recv, local, near, up_s, up_r, down_s, down_r, y_s, y_r = refs[nh:]
     me, blk = lax.axis_index("head"), lax.axis_index("blk")
     greet(nh, nblk, whole, me, blk)
     rows = q.shape[0]
@@ -312,6 +370,16 @@
             pass_on(j, 0)
     start(4)
     start(5)
+
+    def cut(m, which):
+        at = aligned(lax.rem(me + m, nh) * 2 + 1, qc)
+        return pltpu.make_async_copy(
+            (q, g)[which].at[:, at], cuts[m].at[:, pl.ds(which * qc, qc)], near.at[m, which]
+        )
+
+    for m in range(nh):
+        for which in range(2):
+            cut(m, which).start()
     if whole:
         for d in range(1, nz):
             pass_on(0, d)
@@ -328,6 +396,9 @@
                 pl.when(jnp.logical_and(hi + d < nz, hi > 0))(
                     lambda j=j, d=d: down(j, d).wait_send()
                 )
+    for m in range(nh):
+        for which in range(2):
+            cut(m, which).wait()
     arrived(4)
     arrived(5)
     for n in range(6):
@@ -336,7 +407,7 @@
 
 
 def leave(
-    nh, nblk, whole, o0, r1, r2, r3, o1, d0, y0, d1, attn, dq, dk, dv,
+    nh, nblk, whole, o0, r1, r2, r3, o1, d0, y0, d1, far, attn, dq, dk, dv,
     y_in, up_in, down_in, sums, home, send, recv, local, near,
     up_s, up_r, down_s, down_r, y_s, y_r,
 ):
@@ -381,7 +452,7 @@
 
     def across(z):
         return remote(
-            d1.at[aligned(nz + z, group), :], y_in.at[z], (y_s.at[z], y_r.at[z]),
+            far.at[pl.ds(z * group, group), :], y_in.at[z], (y_s.at[z], y_r.at[z]),
             (me, blk + 1 - 2 * lo),
         )
 
@@ -394,85 +465,69 @@
             for which in range(2):
                 brought(m, which).start()
 
-    def up(z):
-        return remote(sums.at[z], up_in.at[z], (up_s.at[z], up_r.at[z]), (me, blk + LINE))
-
-    def down(z):
+    def up(z, j):
         return remote(
-            sums.at[z], down_in.at[z], (down_s.at[z], down_r.at[z]), (me, blk - LINE)
-        )
-
-    def keep(z, value):
-        for j in range(2):
-            sums[z, j] = value[j].astype(bf16)
-
-    def mine(z):
+            sums.at[z, j], up_in.at[z, j], (up_s.at[z, j], up_r.at[z, j]), (me, blk + LINE)
+        )
+
+    def down(z, j):
+        return remote(
+            sums.at[z, j], down_in.at[z, j], (down_s.at[z, j], down_r.at[z, j]),
+            (me, blk - LINE),
+        )
+
+    def mine(z, j):
         at = pl.ds(z * group, group)
-        return [
-            d0[at, :].astype(f32) + y0[at, :].astype(f32),
-            d1[at, :].astype(f32) + y_in[z].astype(f32),
-        ]
-
-    def with_in(value, arrived, z):
-        return [value[j] + arrived[z, j].astype(f32) for j in range(2)]
-
-    def finish(value):
-        for j in range(2):
-            for which in range(2):
-                at = which * 2 + j
-                home[:, at * HEAD_SIZE : (at + 1) * HEAD_SIZE] = value[j][
-                    :, which * HEAD_SIZE : (which + 1) * HEAD_SIZE
-                ].astype(bf16)
+        came = y0[at, :] if j == 0 else y_in[z]
+        return grads[j][at, :].astype(f32) + came.astype(f32)
+
+    def finish(j, value):
+        for which in range(2):
+            at = which * 2 + j
+            home[:, at * HEAD_SIZE : (at + 1) * HEAD_SIZE] = value[
+                :, which * HEAD_SIZE : (which + 1) * HEAD_SIZE
+            ].astype(bf16)
+
+    def hop(z, j, copy, first, arrivals):
+        @pl.when(hi == first)
+        def _():
+            sums[z, j] = mine(z, j).astype(bf16)
+
+        @pl.when(hi != first)
+        def _():
+            copy(z, j).wait_recv()
+            sums[z, j] = (mine(z, j) + arrivals[z, j].astype(f32)).astype(bf16)
+
+        copy(z, j).start()
 
     if whole:
         far_first = sorted(range(nz), key=lambda z: -abs(2 * z - nz + 1))
         for z in far_first:
             across(z).start()
         start_outs()
-        for z in far_first:
-            across(z).wait_recv()
-
-            @pl.when(hi < z)
-            def _(z=z):
-                @pl.when(hi == 0)
-                def _():
-                    keep(z, mine(z))
-
-                @pl.when(hi > 0)
-                def _():
-                    up(z).wait_recv()
-                    keep(z, with_in(mine(z), up_in, z))
-
-                up(z).start()
-
-            @pl.when(hi > z)
-            def _(z=z):
-                @pl.when(hi == nz - 1)
-                def _():
-                    keep(z, mine(z))
-
-                @pl.when(hi < nz - 1)
-                def _():
-                    down(z).wait_recv()
-                    keep(z, with_in(mine(z), down_in, z))
-
-                down(z).start()
-
-        for z in range(nz):
-            @pl.when(hi == z)
-            def _(z=z):
-                value = mine(z)
-                if z > 0:
-                    up(z).wait_recv()
-                    value = with_in(value, up_in, z)
-                if z < nz - 1:
-                    down(z).wait_recv()
-                    value = with_in(value, down_in, z)
-                finish(value)
+        for j in range(2):
+            for z in far_first:
+                if j == 1:
+                    across(z).wait_recv()
+                pl.when(hi < z)(functools.partial(hop, z, j, up, 0, up_in))
+                pl.when(hi > z)(functools.partial(hop, z, j, down, nz - 1, down_in))
+        for j in range(2):
+            for z in range(nz):
+                @pl.when(hi == z)
+                def _(z=z, j=j):
+                    value = mine(z, j)
+                    if z > 0:
+                        up(z, j).wait_recv()
+                        value += up_in[z, j].astype(f32)
+                    if z < nz - 1:
+                        down(z, j).wait_recv()
+                        value += down_in[z, j].astype(f32)
+                    finish(j, value)
 
     else:
         start_outs()
-        finish([grads[j][...].astype(f32) for j in range(2)])
+        for j in range(2):
+            finish(j, grads[j][...].astype(f32))
     for n in (2, 3):
         for m in order:
             to_peer(n, m).start()
@@ -480,8 +535,9 @@
     if whole:
         for z in range(nz):
             across(z).wait_send()
-            pl.when(hi < z)(lambda z=z: up(z).wait_send())
-            pl.when(hi > z)(lambda z=z: down(z).wait_send())
+            for j in range(2):
+                pl.when(hi < z)(lambda z=z, j=j: up(z, j).wait_send())
+                pl.when(hi > z)(lambda z=z, j=j: down(z, j).wait_send())
     for n in range(4):
         for m in order:
             to_peer(n, m).wait()
@@ -516,38 +572,25 @@
     width = query.shape[1] // KEY_VALUE_HEADS
     pair = 2 * HEAD_SIZE
     like = jax.ShapeDtypeStruct
-    q0, g0, kv0, kv1 = pl.pallas_call(
+    q0, g0, kv0, kv1, *cuts = pl.pallas_call(
         functools.partial(enter, nh, nblk, whole),
         out_shape=(
             like((group, width), bf16),
             like((group, width), bf16),
             like((group * (nblk if whole else 1), pair), bf16),
             like((group * (nz if whole else 1), pair), bf16),
-        ),
+        )
+        + (like((rows, 2 * width), bf16),) * nh,
         in_specs=[anywhere] * 4,
-        out_specs=[anywhere] * 4,
+        out_specs=[anywhere] * (4 + nh),
         scratch_shapes=[
-            dma((6, nh - 1)), dma((6, nh - 1)), dma((6,)),
+            dma((6, nh - 1)), dma((6, nh - 1)), dma((6,)), dma((nh, 2)),
             dma((2, nz)), dma((2, nz)), dma((2, nz)), dma((2, nz)),
             dma((2 * nz,)), dma((2 * nz,)),
         ],
         compiler_params=pltpu.CompilerParams(collective_id=0, has_side_effects=True),
     )(query, key, value, output_gradient)
-    query, output_gradient, q0, g0, kv0, kv1 = lax.optimization_barrier(
-        (query, output_gradient, q0, g0, kv0, kv1)
-    )
     me = lax.axis_index("head")
-
-    def second(m):
-        at = (lax.rem(me + m, nh) * 2 + 1) * width
-        return jnp.concatenate(
-            [
-                lax.dynamic_slice_in_dim(x, at, width, 1)
-                for x in (query, output_gradient)
-            ],
-            axis=1,
-        )
-
     if whole:
         kv1 = jnp.concatenate([kv1, swapped(kv1)], axis=0)
     else:
@@ -557,9 +600,7 @@
             )
             for kv in (kv0, kv1)
         )
-    qg1 = jnp.concatenate(
-        [second(0)] + [permuted(second(m), "head", m) for m in range(1, nh)], axis=0
-    )
+    qg1 = [cuts[0]] + [permuted(cuts[m], "head", m) for m in range(1, nh)]
     start = lax.axis_index("blk") if whole else jnp.int32(0)
     base0 = jnp.stack([start, jnp.int32(0), jnp.int32(1)]).astype(jnp.int32)
     base1 = jnp.stack([start, me, jnp.int32(nh - 1)]).astype(jnp.int32)
@@ -573,18 +614,17 @@
             total += permuted(parts[i], "blk", i - nstep).astype(jnp.float32)
         return total.astype(bf16)
 
-    o0, d0 = attention(whole, base0, codes, counts, q0, g0, kv0)
+    o0, *d0 = attention(whole, base0, codes, counts, [q0, g0], kv0)
     came = [
         permuted(
             lax.dynamic_slice_in_dim(o0, lax.rem(me + m, nh) * rows, rows, 0), "head", m
         )
         for m in range(1, nh)
     ]
-    y0 = swapped(d0[nz * group :]) if whole else d0
-    d0 = returned(d0)
-    o1, d1 = attention(whole, base1, codes, counts, qg1, qg1, kv1)
-    d1 = returned(d1)
-    y0 = y0 if whole else d0
+    y0 = swapped(d0[1]) if whole else returned(d0[0])
+    o1, *d1 = attention(whole, base1, codes, counts, qg1, kv1)
+    if not whole:
+        d0, d1 = [y0], [returned(d1[0])]
     y_slots = (nz if whole else 1, group, pair)
     slots = (nz if whole else 1, 2, group, pair)
     return pl.pallas_call(
@@ -593,19 +633,19 @@
             like(query.shape, bf16), like(query.shape, bf16),
             like(key.shape, bf16), like(value.shape, bf16),
         ),
-        in_specs=[anywhere] * 5 + [in_vmem] * 3,
+        in_specs=[anywhere] * 5 + [in_vmem] * 4,
         out_specs=[anywhere] * 4,
         scratch_shapes=[
             pltpu.VMEM(y_slots, bf16), pltpu.VMEM(slots, bf16), pltpu.VMEM(slots, bf16),
             pltpu.VMEM(slots, bf16), pltpu.VMEM((group, 2 * pair), bf16),
             dma((4, nh - 1)), dma((4, nh - 1)), dma((4,)), dma((nh, 2)),
-            dma((nz,)), dma((nz,)), dma((nz,)), dma((nz,)),
+            dma((nz, 2)), dma((nz, 2)), dma((nz, 2)), dma((nz, 2)),
             dma((nz,)), dma((nz,)),
         ],
         compiler_params=pltpu.CompilerParams(
             collective_id=1, has_side_effects=True, vmem_limit_bytes=40 * 2**20
         ),
-    )(o0, *came, o1, d0, y0, d1)
+    )(o0, *came, o1, d0[0], y0, d1[0], d1[-1])
 
 
 def solution(mesh):

time: 211 us -> 232 us (1.100)
  Pallas kernels: 183 us -> 214 us
  local copies, waits for them, and re-layouts: 12.8 us -> 8.06 us
  other arithmetic: 7.25 us -> 2.83 us
    pallas_call x1, Pallas kernels: 45.4 us -> 92.9 us  [body(): pl.pallas_call(functools.partial(enter, nh, nblk, whole), out_shape=(like...]
    pallas_call x2, Pallas kernels: 67.5 us -> 58.7 us  [attention(): pl.pallas_call(functools.partial(attend, nstep, nblocks, heads, split, in...]
    pallas_call x1, Pallas kernels: 70.4 us -> 62.2 us  [body(): pl.pallas_call(functools.partial(leave, nh, nblk, whole), out_shape=(like...]
    concatenate x4 -> x0, other arithmetic: 5.74 us -> none  [the longest x1 3.14 us: body(): jnp.concatenate([second(0)] + [permuted(second(m), 'head', m) for m in ra...]
    unnamed x26 -> x18, local copies, waits for them, and re-layouts: 9.51 us -> 6.51 us
  transfers between devices with their start and end apart: 8 -> 8, of which waited for: 0 -> 0; matrix products, arithmetic and copies ran while one was open for 5% -> 2% of each run, Pallas kernels for 32% -> 25%
where the time goes in v1:
time: 232 us; the launch traced here: 230 us
  Pallas kernels  214 us (92%)
  local copies, waits for them, and re-layouts  8.06 us (3%)
  starting transfers between devices  4.7 us (2%)
  other arithmetic  2.83 us (1%)
    pallas_call x1, Pallas kernels, body(): pl.pallas_call(functools.partial(enter, nh, nblk, whole), out_shape=(like...  92.9 us
    pallas_call x1, Pallas kernels, body(): pl.pallas_call(functools.partial(leave, nh, nblk, whole), out_shape=(like...  62.2 us
    pallas_call x2, Pallas kernels, attention(): pl.pallas_call(functools.partial(attend, nstep, nblocks, heads, split, in...  58.7 us
    unnamed x18, local copies, waits for them, and re-layouts  6.51 us
  transfers between devices with their start and end apart: 8, of which 0 were waited for; matrix products, arithmetic and copies ran while one was open for 2% of the time, Pallas kernels for 25%

profile of v1, /device:TPU:9, one launch (start us, length us, event | category | flops | bytes accessed | tf_op | source)
XLA Modules:
  0.0 230.1 jit_solution(9775025735739759729)
XLA Ops:
  0.6 0.0 copy-start.5
  0.6 0.0 copy-start.4
  0.7 92.9 %shard_map.93 = (bf16[512,1024]{1,0:T(8,128)(2,1)}, bf16[512,1024]{1,0:T(8,128)(2,1)}, bf16[4096,256]{1,0:T(8,128)(2,1)}, bf16[2048,256]{1,0:T(8,128)(2,1)}, bf1...) custom-call(bf16[128,8192]{1,0:T(8,128)(2,1)} %q.1, ...), custom_call_target="tpu_custom_call" | custom-call | tf_op jit(solution)/shard_map/pallas_call | solution.py:575
  93.5 0.5 collective-permute-start.3
  94.1 1.2 collective-permute-start.4
  95.3 0.0 collective-permute-start.5
  95.3 0.3 collective-permute-start.6
  95.6 0.1 pad_add_fusion.base_ref
  95.7 0.0 copy-done.5
  95.7 0.0 copy-done.4
  95.7 0.0 copy-start.1
  95.7 1.2 copy-done.1
  96.9 0.0 copy-start.2
  96.9 1.2 copy-done.2
  98.1 29.0 %shard_map.94 = (bf16[512,2048]{1,0:T(8,128)(2,1)}, bf16[2048,256]{1,0:T(8,128)(2,1)S(1)}, bf16[2048,256]{1,0:T(8,128)(2,1)S(1)}) custom-call(s32[3]{0:T(128)S(1)} %pad_add_fusion.base_ref, s32[8,8]{1,0:T(8,128)S(1)} %bitcast.4, s32[8]{0:T(128)S(1)} %bitcast.6, bf16[512,1024]{1,0:T(8,128)(2,1)S(1)} %copy-done.1, bf16[512,1024]{1,0:T(8,128)(2,1)S(1)} %copy-done.2, ...), custom_call_target="tpu_custom_call" | custom-call | flops 96636764160 | bytes 8388608 | tf_op jit(solution)/shard_map/pallas_call | solution.py:217
  127.1 0.0 collective-permute-start.7
  127.1 0.0 copy-start.6
  127.1 1.5 constant_dynamic-slice_fusion
  128.7 0.1 pad_add_fusion.1.base_ref
  128.7 0.0 collective-permute-done.6
  128.7 0.0 copy-start.3
  128.7 0.9 collective-permute-start.2
  129.7 0.0 copy-done.6
  129.7 2.7 %pad_maximum_fusion.refs_4_.refs_5_ = bf16[4096,256]{1,0:T(8,128)(2,1)} fusion(bf16[2048,256]{1,0:T(8,128)(2,1)} %collective-permute-done.6, bf16[2048,256]{1,0:T(8,128)(2,1)S(1)} %copy-done.6), kind=kLoop, calls=%fused_computation | loop fusion | flops 4194304 | bytes 4194304 | tf_op jit(solution)/shard_map/concatenate | solution.py:595
  132.4 0.0 collective-permute-done.3.refs_1_
  132.4 1.2 collective-permute-start.1
  133.6 0.0 collective-permute-done.4.refs_2_
  133.6 0.5 collective-permute-start
  134.1 0.0 collective-permute-done.5.refs_3_
  134.1 0.0 copy-done.3
  134.1 0.0 copy-start
  134.1 29.7 %shard_map.95 = (bf16[512,2048]{1,0:T(8,128)(2,1)}, bf16[2048,256]{1,0:T(8,128)(2,1)S(1)}, bf16[2048,256]{1,0:T(8,128)(2,1)S(1)}) custom-call(s32[3]{0:T(128)S(1)} %pad_add_fusion.1.base_ref, s32[8,8]{1,0:T(8,128)S(1)} %bitcast.5, s32[8]{0:T(128)S(1)} %bitcast.7, bf16[128,2048]{1,0:T(8,128)(2,1)S(1)} %copy-done.3, ...), custom_call_target="tpu_custom_call" | custom-call | flops 96636764160 | bytes 8388608 | tf_op jit(solution)/shard_map/pallas_call | solution.py:217
  163.8 0.0 collective-permute-done.2.r3
  163.8 0.0 collective-permute-done.1.r2
  163.8 0.0 collective-permute-done.r1
  163.8 0.0 collective-permute-done.7.y0
  163.8 0.0 copy-done
  163.8 62.2 %shard_map.96 = (bf16[128,8192]{1,0:T(8,128)(2,1)S(1)}, bf16[128,8192]{1,0:T(8,128)(2,1)S(1)}, bf16[128,1024]{1,0:T(8,128)(2,1)S(1)}, bf16[128,1024]{1,0:T(8,128)(2,1)S(1)}) custom-call(bf16[512,2048]{1,0:T(8,128)(2,1)S(1)} %copy-done, bf16[128,2048]{1,0:T(8,128)(2,1)S(1)} %collective-permute-done.r1, bf16[128,2048]{1,0:T(8,128)(2,1)S(1)} %collective-permute-done.1.r2, ...), custom_call_target="tpu_custom_call" | custom-call | tf_op jit(solution)/shard_map/pallas_call | solution.py:630
  226.0 1.3 copy.14
  227.4 1.3 copy.15
  228.7 0.7 copy.16
  229.4 0.7 copy.17
Async XLA Ops:
  0.6 95.0 %copy-start.5 = (s32[1,8]{1,0:T(1,128)S(1)}, s32[1,8]{1,0:T(1,128)}, u32[]{:S(2)}) copy-start(s32[1,8]{1,0:T(1,128)} %param.11) | copy-start | bytes 100
  0.6 95.0 %copy-start.4 = (s32[1,8,8]{2,1,0:T(8,128)S(1)}, s32[1,8,8]{2,1,0:T(8,128)}, u32[]{:S(2)}) copy-start(s32[1,8,8]{2,1,0:T(8,128)} %param.10) | copy-start | bytes 772
  93.5 38.8 %collective-permute-start.3 = (bf16[128,2048]{1,0:T(8,128)(2,1)}, bf16[128,2048]{1,0:T(8,128)(2,1)}, u32[]{:S(2)}, u32[]{:S(2)}) collective-permute-start(bf16[128,2048]{1,0:T(8,128)(2,1)} %get-tuple-element.23), channel_id=1, source_target_pairs={{0,8},{8,16},{16,24},{24,0},{1,9},{9,17},{17,25},{25,1},{2,10},{10... | collective-permute-start | bytes 1572872 | tf_op jit(solution)/shard_map/ppermute | solution.py:552
  94.1 39.5 %collective-permute-start.4 = (bf16[128,2048]{1,0:T(8,128)(2,1)}, bf16[128,2048]{1,0:T(8,128)(2,1)}, u32[]{:S(2)}, u32[]{:S(2)}) collective-permute-start(bf16[128,2048]{1,0:T(8,128)(2,1)} %get-tuple-element.24), channel_id=1, source_target_pairs={{0,16},{8,24},{16,0},{24,8},{1,17},{9,25},{17,1},{25,9},{2,18},{10... | collective-permute-start | bytes 1572872 | tf_op jit(solution)/shard_map/ppermute | solution.py:552
  95.3 38.8 %collective-permute-start.5 = (bf16[128,2048]{1,0:T(8,128)(2,1)}, bf16[128,2048]{1,0:T(8,128)(2,1)}, u32[]{:S(2)}, u32[]{:S(2)}) collective-permute-start(bf16[128,2048]{1,0:T(8,128)(2,1)} %get-tuple-element.25), channel_id=1, source_target_pairs={{0,24},{8,0},{16,8},{24,16},{1,25},{9,1},{17,9},{25,17},{2,26},{10... | collective-permute-start | bytes 1572872 | tf_op jit(solution)/shard_map/ppermute | solution.py:552
  95.3 33.4 %collective-permute-start.6 = (bf16[2048,256]{1,0:T(8,128)(2,1)}, bf16[2048,256]{1,0:T(8,128)(2,1)}, u32[]{:S(2)}, u32[]{:S(2)}) collective-permute-start(bf16[2048,256]{1,0:T(8,128)(2,1)} %get-tuple-element.26), channel_id=1, source_target_pairs={{0,1},{1,0},{2,3},{3,2},{4,5},{5,4},{6,7},{7,6},{8,9},{9,8},{10,11... | collective-permute-start | bytes 3145736 | tf_op jit(solution)/shard_map/ppermute | solution.py:556
  95.7 1.2 copy-start.1
  96.9 1.2 copy-start.2
  127.1 36.7 %collective-permute-start.7 = (bf16[2048,256]{1,0:T(8,128)(2,1)S(1)}, bf16[2048,256]{1,0:T(8,128)(2,1)S(1)}, u32[]{:S(2)}, u32[]{:S(2)}) collective-permute-start(bf16[2048,256]{1,0:T(8,128)(2,1)S(1)} %get-tuple-element.29), channel_id=1, source_target_pairs={{0,1},{1,0},{2,3},{3,2},{4,5},{5,4},{6,7},{7,6},{8,9},{9,8},{10,11... | collective-permute-start | bytes 3145736 | tf_op jit(solution)/shard_map/ppermute | solution.py:556
  127.1 2.6 %copy-start.6 = (bf16[2048,256]{1,0:T(8,128)(2,1)S(1)}, bf16[2048,256]{1,0:T(8,128)(2,1)}, u32[]{:S(2)}) copy-start(bf16[2048,256]{1,0:T(8,128)(2,1)} %get-tuple-element.26) | copy-start | bytes 3145732
  128.7 5.4 %copy-start.3 = (bf16[128,2048]{1,0:T(8,128)(2,1)S(1)}, bf16[128,2048]{1,0:T(8,128)(2,1)}, u32[]{:S(2)}) copy-start(bf16[128,2048]{1,0:T(8,128)(2,1)} %get-tuple-element.22.refs_0_) | copy-start | bytes 1572868
  128.7 35.0 %collective-permute-start.2 = (bf16[128,2048]{1,0:T(8,128)(2,1)S(1)}, bf16[128,2048]{1,0:T(8,128)(2,1)S(1)}, u32[]{:S(2)}, u32[]{:S(2)}) collective-permute-start(bf16[128,2048]{1,0:T(8,128)(2,1)S(1)} %get-tuple-element.32), channel_id=1, source_target_pairs={{0,24},{8,0},{16,8},{24,16},{1,25},{9,1},{17,9},{25,17},{2,26},{10... | collective-permute-start | bytes 1572872 | tf_op jit(solution)/shard_map/ppermute | solution.py:552
  132.4 31.4 %collective-permute-start.1 = (bf16[128,2048]{1,0:T(8,128)(2,1)S(1)}, bf16[128,2048]{1,0:T(8,128)(2,1)S(1)}, u32[]{:S(2)}, u32[]{:S(2)}) collective-permute-start(bf16[128,2048]{1,0:T(8,128)(2,1)S(1)} %get-tuple-element.33), channel_id=1, source_target_pairs={{0,16},{8,24},{16,0},{24,8},{1,17},{9,25},{17,1},{25,9},{2,18},{10... | collective-permute-start | bytes 1572872 | tf_op jit(solution)/shard_map/ppermute | solution.py:552
  133.6 30.2 %collective-permute-start = (bf16[128,2048]{1,0:T(8,128)(2,1)S(1)}, bf16[128,2048]{1,0:T(8,128)(2,1)S(1)}, u32[]{:S(2)}, u32[]{:S(2)}) collective-permute-start(bf16[128,2048]{1,0:T(8,128)(2,1)S(1)} %get-tuple-element.34), channel_id=1, source_target_pairs={{0,8},{8,16},{16,24},{24,0},{1,9},{9,17},{17,25},{25,1},{2,10},{10... | collective-permute-start | bytes 1572872 | tf_op jit(solution)/shard_map/ppermute | solution.py:552
  134.1 29.7 %copy-start = (bf16[512,2048]{1,0:T(8,128)(2,1)S(1)}, bf16[512,2048]{1,0:T(8,128)(2,1)}, u32[]{:S(2)}) copy-start(bf16[512,2048]{1,0:T(8,128)(2,1)} %get-tuple-element.21.o0) | copy-start | bytes 6291460

commit v2 on v1

--- a/solution.py
+++ b/solution.py
@@ -281,7 +281,7 @@
     nh, nblk, whole, q, k, v, g, q0, g0, kv0, kv1, *refs
 ):
     cuts = refs[:nh]
-    send, recv, local, near, up_s, up_r, down_s, down_r, y_s, y_r = refs[nh:]
+    send, recv, up_s, up_r, down_s, down_r, y_s, y_r = refs[nh:]
     me, blk = lax.axis_index("head"), lax.axis_index("blk")
     greet(nh, nblk, whole, me, blk)
     rows = q.shape[0]
@@ -309,19 +309,17 @@
 
     def own(n):
         src, cols, j, dst = parts(n)
-        return pltpu.make_async_copy(src.at[:, aligned(me * 2 + j, cols)], dst, local.at[n])
+        dst[...] = src[:, aligned(me * 2 + j, cols)]
 
     order = (2, 3, 1) if nh == 4 else tuple(range(1, nh))
 
     def start(n):
         for m in order:
             to_peer(n, m).start()
-        own(n).start()
 
     def arrived(n):
         for m in order:
             to_peer(n, m).wait_recv()
-        own(n).wait()
 
     def block(j, z):
         return keys[j].at[aligned(z, group), :]
@@ -363,6 +361,8 @@
 
     for n in range(4):
         start(n)
+    for n in range(4):
+        own(n)
     for j in range(2):
         arrived(2 * j)
         arrived(2 * j + 1)
@@ -371,15 +371,12 @@
     start(4)
     start(5)
 
-    def cut(m, which):
+    own(4)
+    own(5)
+    for m in range(nh):
         at = aligned(lax.rem(me + m, nh) * 2 + 1, qc)
-        return pltpu.make_async_copy(
-            (q, g)[which].at[:, at], cuts[m].at[:, pl.ds(which * qc, qc)], near.at[m, which]
-        )
-
-    for m in range(nh):
-        for which in range(2):
-            cut(m, which).start()
+        cuts[m][:, :qc] = q[:, at]
+        cuts[m][:, qc:] = g[:, at]
     if whole:
         for d in range(1, nz):
             pass_on(0, d)
@@ -396,9 +393,6 @@
                 pl.when(jnp.logical_and(hi + d < nz, hi > 0))(
                     lambda j=j, d=d: down(j, d).wait_send()
                 )
-    for m in range(nh):
-        for which in range(2):
-            cut(m, which).wait()
     arrived(4)
     arrived(5)
     for n in range(6):
@@ -408,7 +402,7 @@
 
 def leave(
     nh, nblk, whole, o0, r1, r2, r3, o1, d0, y0, d1, far, attn, dq, dk, dv,
-    y_in, up_in, down_in, sums, home, send, recv, local, near,
+    y_in, up_in, down_in, sums, home, send, recv,
     up_s, up_r, down_s, down_r, y_s, y_r,
 ):
     me, blk = lax.axis_index("head"), lax.axis_index("blk")
@@ -440,13 +434,13 @@
 
     def own(n):
         src, dst = part(n, me)
-        return pltpu.make_async_copy(src, dst, local.at[n])
+        dst[...] = src[...]
 
     def brought(m, which):
         cols = pl.ds(which * half, half)
         src = o0.at[aligned(me, rows), cols] if m == 0 else (r1, r2, r3)[m - 1].at[:, cols]
-        dst = (attn, dq)[which].at[:, aligned(lax.rem(me - m + nh, nh) * 2, half)]
-        return pltpu.make_async_copy(src, dst, near.at[m, which])
+        to = aligned(lax.rem(me - m + nh, nh) * 2, half)
+        (attn, dq)[which][:, to] = src[...]
 
     order = (2, 3, 1) if nh == 4 else tuple(range(1, nh))
 
@@ -460,10 +454,13 @@
         for n in range(2):
             for m in order:
                 to_peer(n, m).start()
-            own(n).start()
+
+    def bring_outs():
+        for n in range(2):
+            own(n)
         for m in range(nh):
             for which in range(2):
-                brought(m, which).start()
+                brought(m, which)
 
     def up(z, j):
         return remote(
@@ -531,7 +528,8 @@
     for n in (2, 3):
         for m in order:
             to_peer(n, m).start()
-        own(n).start()
+        own(n)
+    bring_outs()
     if whole:
         for z in range(nz):
             across(z).wait_send()
@@ -541,10 +539,6 @@
     for n in range(4):
         for m in order:
             to_peer(n, m).wait()
-        own(n).wait()
-    for m in range(nh):
-        for which in range(2):
-            brought(m, which).wait()
 
 
 def permuted(block, axis, distance):
@@ -567,7 +561,6 @@
     group = nh * rows
     bf16 = jnp.bfloat16
     dma = pltpu.SemaphoreType.DMA
-    anywhere = pl.BlockSpec(memory_space=pl.ANY)
     in_vmem = pl.BlockSpec(memory_space=pltpu.VMEM)
     width = query.shape[1] // KEY_VALUE_HEADS
     pair = 2 * HEAD_SIZE
@@ -581,14 +574,16 @@
             like((group * (nz if whole else 1), pair), bf16),
         )
         + (like((rows, 2 * width), bf16),) * nh,
-        in_specs=[anywhere] * 4,
-        out_specs=[anywhere] * (4 + nh),
+        in_specs=[in_vmem] * 4,
+        out_specs=[in_vmem] * (4 + nh),
         scratch_shapes=[
-            dma((6, nh - 1)), dma((6, nh - 1)), dma((6,)), dma((nh, 2)),
+            dma((6, nh - 1)), dma((6, nh - 1)),
             dma((2, nz)), dma((2, nz)), dma((2, nz)), dma((2, nz)),
             dma((2 * nz,)), dma((2 * nz,)),
         ],
-        compiler_params=pltpu.CompilerParams(collective_id=0, has_side_effects=True),
+        compiler_params=pltpu.CompilerParams(
+            collective_id=0, has_side_effects=True, vmem_limit_bytes=40 * 2**20
+        ),
     )(query, key, value, output_gradient)
     me = lax.axis_index("head")
     if whole:
@@ -633,12 +628,12 @@
             like(query.shape, bf16), like(query.shape, bf16),
             like(key.shape, bf16), like(value.shape, bf16),
         ),
-        in_specs=[anywhere] * 5 + [in_vmem] * 4,
-        out_specs=[anywhere] * 4,
+        in_specs=[in_vmem] * 9,
+        out_specs=[in_vmem] * 4,
         scratch_shapes=[
             pltpu.VMEM(y_slots, bf16), pltpu.VMEM(slots, bf16), pltpu.VMEM(slots, bf16),
             pltpu.VMEM(slots, bf16), pltpu.VMEM((group, 2 * pair), bf16),
-            dma((4, nh - 1)), dma((4, nh - 1)), dma((4,)), dma((nh, 2)),
+            dma((4, nh - 1)), dma((4, nh - 1)),
             dma((nz, 2)), dma((nz, 2)), dma((nz, 2)), dma((nz, 2)),
             dma((nz,)), dma((nz,)),
         ],

time: 232 us -> 198 us (0.85)
  Pallas kernels: 214 us -> 170 us
  local copies, waits for them, and re-layouts: 8.06 us -> 14.9 us
  starting transfers between devices: 4.7 us -> 9.4 us
    pallas_call x1, Pallas kernels: 92.9 us -> 45.8 us  [body(): pl.pallas_call(functools.partial(enter, nh, nblk, whole), out_shape=(like...]
    pallas_call x1, Pallas kernels: 62.2 us -> 72.5 us  [body(): pl.pallas_call(functools.partial(leave, nh, nblk, whole), out_shape=(like...]
    unnamed x18 -> x28, local copies, waits for them, and re-layouts: 6.51 us -> 13.4 us
    pallas_call x2, Pallas kernels: 58.7 us -> 52.1 us  [attention(): pl.pallas_call(functools.partial(attend, nstep, nblocks, heads, split, in...]
    ppermute x2, starting transfers between devices: 0.3 us -> 4.92 us  [swapped(): lax.ppermute(block, 'blk', [(i, i ^ 1) for i in range(lax.axis_size('blk'...]
  transfers between devices with their start and end apart: 8 -> 8, of which waited for: 0 -> 0; matrix products, arithmetic and copies ran while one was open for 2% -> 2% of each run, Pallas kernels for 25% -> 26%
where the time goes in v2:
time: 198 us
  Pallas kernels  170 us (86%)
  local copies, waits for them, and re-layouts  14.9 us (8%)
  starting transfers between devices  9.4 us (5%)
  other arithmetic  2.83 us (1%)
    pallas_call x1, Pallas kernels, body(): pl.pallas_call(functools.partial(leave, nh, nblk, whole), out_shape=(like...  72.5 us
    pallas_call x2, Pallas kernels, attention(): pl.pallas_call(functools.partial(attend, nstep, nblocks, heads, split, in...  52.1 us
    pallas_call x1, Pallas kernels, body(): pl.pallas_call(functools.partial(enter, nh, nblk, whole), out_shape=(like...  45.8 us
    unnamed x28, local copies, waits for them, and re-layouts  13.4 us
    ppermute x2, starting transfers between devices, swapped(): lax.ppermute(block, 'blk', [(i, i ^ 1) for i in range(lax.axis_size('blk'...  4.92 us
    ppermute x6, starting transfers between devices, permuted(): lax.ppermute(block, axis, [(i, (i + distance) % size) for i in range(size)])  4.49 us
  transfers between devices with their start and end apart: 8, of which 0 were waited for; matrix products, arithmetic and copies ran while one was open for 2% of the time, Pallas kernels for 26%

profile of v2, /device:TPU:9, one launch (start us, length us, event | category | flops | bytes accessed | tf_op | source)
XLA Modules:
  0.0 198.2 jit_solution(12161103095189617029)
XLA Ops:
  0.6 0.0 copy-start.1
  0.6 1.6 copy-done.1
  2.2 0.0 copy-start.2
  2.2 1.6 copy-done.2
  3.8 0.0 copy-start.3
  3.8 0.9 copy-done.3
  4.8 0.0 copy-start.4
  4.8 0.9 copy-done.4
  5.7 0.0 copy-start.10
  5.7 0.0 copy-start.11
  5.7 45.8 %shard_map.93 = (bf16[512,1024]{1,0:T(8,128)(2,1)S(1)}, bf16[512,1024]{1,0:T(8,128)(2,1)S(1)}, bf16[4096,256]{1,0:T(8,128)(2,1)S(1)}, bf16[2048,256]{1,0:T(8,128...) custom-call(bf16[128,8192]{1,0:T(8,128)(2,1)S(1)} %copy-done.1, ...), custom_call_target="tpu_custom_call" | custom-call | tf_op jit(solution)/shard_map/pallas_call | solution.py:568
  51.5 0.0 copy-start.5
  51.6 1.3 copy-done.5
  52.9 0.0 copy-start.6
  52.9 1.0 copy-done.6
  53.8 0.8 copy-done.8
  54.6 0.4 collective-permute-start.3
  55.0 1.2 collective-permute-start.4
  56.2 0.0 collective-permute-start.5
  56.2 0.3 collective-permute-start.6
  56.5 0.1 pad_add_fusion.base_ref
  56.6 0.0 copy-done.10
  56.6 0.0 copy-done.11
  56.6 1.2 copy-done.7
  57.8 25.9 %shard_map.94 = (bf16[512,2048]{1,0:T(8,128)(2,1)}, bf16[2048,256]{1,0:T(8,128)(2,1)S(1)}, bf16[2048,256]{1,0:T(8,128)(2,1)}) custom-call(s32[3]{0:T(128)S(1)} %pad_add_fusion.base_ref, s32[8,8]{1,0:T(8,128)S(1)} %bitcast.4, s32[8]{0:T(128)S(1)} %bitcast.6, bf16[512,1024]{1,0:T(8,128)(2,1)S(1)} %get-tuple-element.18.refs_0_, ...), custom_call_target="tpu_custom_call" | custom-call | flops 96636764160 | bytes 8388608 | tf_op jit(solution)/shard_map/pallas_call | solution.py:217
  83.7 4.6 %collective-permute-start.7 = (bf16[2048,256]{1,0:T(8,128)(2,1)}, bf16[2048,256]{1,0:T(8,128)(2,1)S(1)}, u32[]{:S(2)}, u32[]{:S(2)}) collective-permute-start(bf16[2048,256]{1,0:T(8,128)(2,1)} %get-tuple-element.29), channel_id=1, source_target_pairs={{0,1},{1,0},{2,3},{3,2},{4,5},{5,4},{6,7},{7,6},{8,9},{9,8},{10,11... | collective-permute-start | bytes 3145736 | tf_op jit(solution)/shard_map/ppermute | solution.py:550
  88.3 1.5 constant_dynamic-slice_fusion
  89.8 0.1 pad_add_fusion.1.base_ref
  89.8 0.0 collective-permute-done.6
  89.8 1.2 collective-permute-start.2
  91.1 2.7 %pad_maximum_fusion.refs_4_.refs_5_ = bf16[4096,256]{1,0:T(8,128)(2,1)} fusion(bf16[2048,256]{1,0:T(8,128)(2,1)} %collective-permute-done.6, bf16[2048,256]{1,0:T(8,128)(2,1)S(1)} %get-tuple-element.26), kind=kLoop, calls=%fused_computation | loop fusion | flops 4194304 | bytes 4194304 | tf_op jit(solution)/shard_map/concatenate | solution.py:590
  93.7 0.0 collective-permute-done.3.refs_1_
  93.7 1.2 collective-permute-start.1
  95.0 0.0 collective-permute-done.4.refs_2_
  95.0 0.5 collective-permute-start
  95.4 0.0 collective-permute-done.5.refs_3_
  95.4 0.0 copy-done.9
  95.5 26.2 %shard_map.95 = (bf16[512,2048]{1,0:T(8,128)(2,1)}, bf16[2048,256]{1,0:T(8,128)(2,1)S(1)}, bf16[2048,256]{1,0:T(8,128)(2,1)S(1)}) custom-call(s32[3]{0:T(128)S(1)} %pad_add_fusion.1.base_ref, s32[8,8]{1,0:T(8,128)S(1)} %bitcast.5, s32[8]{0:T(128)S(1)} %bitcast.7, bf16[128,2048]{1,0:T(8,128)(2,1)S(1)} %copy-done.9, ...), custom_call_target="tpu_custom_call" | custom-call | flops 96636764160 | bytes 8388608 | tf_op jit(solution)/shard_map/pallas_call | solution.py:217
  121.6 0.0 collective-permute-done.2.r3
  121.7 0.0 collective-permute-done.1.r2
  121.7 0.0 collective-permute-done.r1
  121.7 0.0 collective-permute-done.7.y0
  121.7 0.0 copy-done
  121.7 72.5 %shard_map.96 = (bf16[128,8192]{1,0:T(8,128)(2,1)S(1)}, bf16[128,8192]{1,0:T(8,128)(2,1)S(1)}, bf16[128,1024]{1,0:T(8,128)(2,1)S(1)}, bf16[128,1024]{1,0:T(8,128)(2,1)S(1)}) custom-call(bf16[512,2048]{1,0:T(8,128)(2,1)S(1)} %copy-done, bf16[128,2048]{1,0:T(8,128)(2,1)S(1)} %collective-permute-done.r1, bf16[128,2048]{1,0:T(8,128)(2,1)S(1)} %collective-permute-done.1.r2, ...), custom_call_target="tpu_custom_call" | custom-call | tf_op jit(solution)/shard_map/pallas_call | solution.py:625
  194.2 1.3 copy.14
  195.5 1.3 copy.15
  196.8 0.7 copy.16
  197.5 0.7 copy.17
  (4 shorter events, 0.0 us)
Async XLA Ops:
  0.6 1.6 copy-start.1
  2.2 1.6 copy-start.2
  3.8 0.9 copy-start.3
  4.8 0.9 copy-start.4
  5.7 50.9 %copy-start.10 = (s32[1,8,8]{2,1,0:T(8,128)S(1)}, s32[1,8,8]{2,1,0:T(8,128)}, u32[]{:S(2)}) copy-start(s32[1,8,8]{2,1,0:T(8,128)} %param.10) | copy-start | bytes 772
  5.7 50.9 %copy-start.11 = (s32[1,8]{1,0:T(1,128)S(1)}, s32[1,8]{1,0:T(1,128)}, u32[]{:S(2)}) copy-start(s32[1,8]{1,0:T(1,128)} %param.11) | copy-start | bytes 100
  51.5 1.3 copy-start.5
  52.9 1.0 copy-start.6
  53.8 0.8 copy-start.8
  54.6 39.1 %collective-permute-start.3 = (bf16[128,2048]{1,0:T(8,128)(2,1)}, bf16[128,2048]{1,0:T(8,128)(2,1)}, u32[]{:S(2)}, u32[]{:S(2)}) collective-permute-start(bf16[128,2048]{1,0:T(8,128)(2,1)} %get-tuple-element.23), channel_id=1, source_target_pairs={{0,8},{8,16},{16,24},{24,0},{1,9},{9,17},{17,25},{25,1},{2,10},{10... | collective-permute-start | bytes 1572872 | tf_op jit(solution)/shard_map/ppermute | solution.py:546
  55.0 40.0 %collective-permute-start.4 = (bf16[128,2048]{1,0:T(8,128)(2,1)}, bf16[128,2048]{1,0:T(8,128)(2,1)}, u32[]{:S(2)}, u32[]{:S(2)}) collective-permute-start(bf16[128,2048]{1,0:T(8,128)(2,1)} %get-tuple-element.24), channel_id=1, source_target_pairs={{0,16},{8,24},{16,0},{24,8},{1,17},{9,25},{17,1},{25,9},{2,18},{10... | collective-permute-start | bytes 1572872 | tf_op jit(solution)/shard_map/ppermute | solution.py:546
  56.2 39.2 %collective-permute-start.5 = (bf16[128,2048]{1,0:T(8,128)(2,1)}, bf16[128,2048]{1,0:T(8,128)(2,1)}, u32[]{:S(2)}, u32[]{:S(2)}) collective-permute-start(bf16[128,2048]{1,0:T(8,128)(2,1)} %get-tuple-element.25), channel_id=1, source_target_pairs={{0,24},{8,0},{16,8},{24,16},{1,25},{9,1},{17,9},{25,17},{2,26},{10... | collective-permute-start | bytes 1572872 | tf_op jit(solution)/shard_map/ppermute | solution.py:546
  56.2 33.6 %collective-permute-start.6 = (bf16[2048,256]{1,0:T(8,128)(2,1)S(1)}, bf16[2048,256]{1,0:T(8,128)(2,1)}, u32[]{:S(2)}, u32[]{:S(2)}) collective-permute-start(bf16[2048,256]{1,0:T(8,128)(2,1)S(1)} %get-tuple-element.26), channel_id=1, source_target_pairs={{0,1},{1,0},{2,3},{3,2},{4,5},{5,4},{6,7},{7,6},{8,9},{9,8},{10,11... | collective-permute-start | bytes 3145736 | tf_op jit(solution)/shard_map/ppermute | solution.py:550
  56.6 1.2 copy-start.7
  83.7 38.0 %collective-permute-start.7 = (bf16[2048,256]{1,0:T(8,128)(2,1)}, bf16[2048,256]{1,0:T(8,128)(2,1)S(1)}, u32[]{:S(2)}, u32[]{:S(2)}) collective-permute-start(bf16[2048,256]{1,0:T(8,128)(2,1)} %get-tuple-element.29), channel_id=1, source_target_pairs={{0,1},{1,0},{2,3},{3,2},{4,5},{5,4},{6,7},{7,6},{8,9},{9,8},{10,11... | collective-permute-start | bytes 3145736 | tf_op jit(solution)/shard_map/ppermute | solution.py:550
  89.8 5.6 %copy-start.9 = (bf16[128,2048]{1,0:T(8,128)(2,1)S(1)}, bf16[128,2048]{1,0:T(8,128)(2,1)}, u32[]{:S(2)}) copy-start(bf16[128,2048]{1,0:T(8,128)(2,1)} %copy-done.8) | copy-start | bytes 1572868
  89.8 31.8 %collective-permute-start.2 = (bf16[128,2048]{1,0:T(8,128)(2,1)S(1)}, bf16[128,2048]{1,0:T(8,128)(2,1)S(1)}, u32[]{:S(2)}, u32[]{:S(2)}) collective-permute-start(bf16[128,2048]{1,0:T(8,128)(2,1)S(1)} %get-tuple-element.32), channel_id=1, source_target_pairs={{0,24},{8,0},{16,8},{24,16},{1,25},{9,1},{17,9},{25,17},{2,26},{10... | collective-permute-start | bytes 1572872 | tf_op jit(solution)/shard_map/ppermute | solution.py:546
  93.7 27.9 %collective-permute-start.1 = (bf16[128,2048]{1,0:T(8,128)(2,1)S(1)}, bf16[128,2048]{1,0:T(8,128)(2,1)S(1)}, u32[]{:S(2)}, u32[]{:S(2)}) collective-permute-start(bf16[128,2048]{1,0:T(8,128)(2,1)S(1)} %get-tuple-element.33), channel_id=1, source_target_pairs={{0,16},{8,24},{16,0},{24,8},{1,17},{9,25},{17,1},{25,9},{2,18},{10... | collective-permute-start | bytes 1572872 | tf_op jit(solution)/shard_map/ppermute | solution.py:546
  95.0 26.7 %collective-permute-start = (bf16[128,2048]{1,0:T(8,128)(2,1)S(1)}, bf16[128,2048]{1,0:T(8,128)(2,1)S(1)}, u32[]{:S(2)}, u32[]{:S(2)}) collective-permute-start(bf16[128,2048]{1,0:T(8,128)(2,1)S(1)} %get-tuple-element.34), channel_id=1, source_target_pairs={{0,8},{8,16},{16,24},{24,0},{1,9},{9,17},{17,25},{25,1},{2,10},{10... | collective-permute-start | bytes 1572872 | tf_op jit(solution)/shard_map/ppermute | solution.py:546
  95.5 26.2 %copy-start = (bf16[512,2048]{1,0:T(8,128)(2,1)S(1)}, bf16[512,2048]{1,0:T(8,128)(2,1)}, u32[]{:S(2)}) copy-start(bf16[512,2048]{1,0:T(8,128)(2,1)} %get-tuple-element.21.o0) | copy-start | bytes 6291460

commit v3 on v2

--- a/solution.py
+++ b/solution.py
@@ -498,16 +498,23 @@
         copy(z, j).start()
 
     if whole:
-        far_first = sorted(range(nz), key=lambda z: -abs(2 * z - nz + 1))
-        for z in far_first:
-            across(z).start()
-        start_outs()
-        for j in range(2):
-            for z in far_first:
-                if j == 1:
-                    across(z).wait_recv()
-                pl.when(hi < z)(functools.partial(hop, z, j, up, 0, up_in))
-                pl.when(hi > z)(functools.partial(hop, z, j, down, nz - 1, down_in))
+        def chains(order):
+            for z in order:
+                across(z).start()
+            start_outs()
+            for j in range(2):
+                for z in order:
+                    if j == 1:
+                        across(z).wait_recv()
+                    pl.when(hi < z)(functools.partial(hop, z, j, up, 0, up_in))
+                    pl.when(hi > z)(functools.partial(hop, z, j, down, nz - 1, down_in))
+
+        def ends_first(places):
+            return [places[i // 2] if i % 2 == 0 else places[-1 - i // 2] for i in range(nz)]
+
+        upward = ends_first(list(range(nz - 1, -1, -1)))
+        pl.when(hi < nz // 2)(functools.partial(chains, upward))
+        pl.when(hi >= nz // 2)(functools.partial(chains, ends_first(list(range(nz)))))
         for j in range(2):
             for z in range(nz):
                 @pl.when(hi == z)

time: 198 us -> 189 us (0.955); the launches traced: 198 us -> 186 us
  Pallas kernels: 170 us -> 162 us
  starting transfers between devices: 9.4 us -> 5.95 us
    pallas_call x1, Pallas kernels: 72.5 us -> 56.9 us  [body(): pl.pallas_call(functools.partial(leave, nh, nblk, whole), out_shape=(like...]
    pallas_call x2, Pallas kernels: 52.1 us -> 59 us  [attention(): pl.pallas_call(functools.partial(attend, nstep, nblocks, heads, split, in...]
    ppermute x2, starting transfers between devices: 4.92 us -> 1.46 us  [swapped(): lax.ppermute(block, 'blk', [(i, i ^ 1) for i in range(lax.axis_size('blk'...]
  transfers between devices with their start and end apart: 8 -> 8, of which waited for: 0 -> 0; matrix products, arithmetic and copies ran while one was open for 2% -> 2% of each run, Pallas kernels for 26% -> 32%
where the time goes in v3:
time: 189 us; the launch traced here: 186 us
  Pallas kernels  162 us (86%)
  local copies, waits for them, and re-layouts  14.9 us (8%)
  starting transfers between devices  5.95 us (3%)
  other arithmetic  2.83 us (1%)
    pallas_call x2, Pallas kernels, attention(): pl.pallas_call(functools.partial(attend, nstep, nblocks, heads, split, in...  59 us
    pallas_call x1, Pallas kernels, body(): pl.pallas_call(functools.partial(leave, nh, nblk, whole), out_shape=(like...  56.9 us
    pallas_call x1, Pallas kernels, body(): pl.pallas_call(functools.partial(enter, nh, nblk, whole), out_shape=(like...  45.8 us
    unnamed x28, local copies, waits for them, and re-layouts  13.4 us
    ppermute x6, starting transfers between devices, permuted(): lax.ppermute(block, axis, [(i, (i + distance) % size) for i in range(size)])  4.49 us
  transfers between devices with their start and end apart: 8, of which 0 were waited for; matrix products, arithmetic and copies ran while one was open for 2% of the time, Pallas kernels for 32%

profile of v3, /device:TPU:9, one launch (start us, length us, event | category | flops | bytes accessed | tf_op | source)
XLA Modules:
  0.0 186.1 jit_solution(5936795585817801865)
XLA Ops:
  0.6 0.0 copy-start.1
  0.6 1.6 copy-done.1
  2.2 0.0 copy-start.2
  2.2 1.6 copy-done.2
  3.8 0.0 copy-start.3
  3.8 0.9 copy-done.3
  4.8 0.0 copy-start.4
  4.8 0.9 copy-done.4
  5.7 0.0 copy-start.10
  5.7 0.0 copy-start.11
  5.7 45.8 %shard_map.93 = (bf16[512,1024]{1,0:T(8,128)(2,1)S(1)}, bf16[512,1024]{1,0:T(8,128)(2,1)S(1)}, bf16[4096,256]{1,0:T(8,128)(2,1)S(1)}, bf16[2048,256]{1,0:T(8,128...) custom-call(bf16[128,8192]{1,0:T(8,128)(2,1)S(1)} %copy-done.1, ...), custom_call_target="tpu_custom_call" | custom-call | tf_op jit(solution)/shard_map/pallas_call | solution.py:575
  51.5 0.0 copy-start.5
  51.6 1.3 copy-done.5
  52.9 0.0 copy-start.6
  52.9 1.0 copy-done.6
  53.8 0.8 copy-done.8
  54.6 0.4 collective-permute-start.3
  55.0 1.2 collective-permute-start.4
  56.2 0.0 collective-permute-start.5
  56.2 0.3 collective-permute-start.6
  56.5 0.1 pad_add_fusion.base_ref
  56.6 0.0 copy-done.10
  56.6 0.0 copy-done.11
  56.6 1.2 copy-done.7
  57.8 29.3 %shard_map.94 = (bf16[512,2048]{1,0:T(8,128)(2,1)}, bf16[2048,256]{1,0:T(8,128)(2,1)S(1)}, bf16[2048,256]{1,0:T(8,128)(2,1)}) custom-call(s32[3]{0:T(128)S(1)} %pad_add_fusion.base_ref, s32[8,8]{1,0:T(8,128)S(1)} %bitcast.4, s32[8]{0:T(128)S(1)} %bitcast.6, bf16[512,1024]{1,0:T(8,128)(2,1)S(1)} %get-tuple-element.18.refs_0_, ...), custom_call_target="tpu_custom_call" | custom-call | flops 96636764160 | bytes 8388608 | tf_op jit(solution)/shard_map/pallas_call | solution.py:217
  87.1 1.2 collective-permute-start.7
  88.3 1.5 constant_dynamic-slice_fusion
  89.7 0.1 pad_add_fusion.1.base_ref
  89.8 0.0 collective-permute-done.6
  89.8 1.2 collective-permute-start.2
  91.0 2.7 %pad_maximum_fusion.refs_4_.refs_5_ = bf16[4096,256]{1,0:T(8,128)(2,1)} fusion(bf16[2048,256]{1,0:T(8,128)(2,1)} %collective-permute-done.6, bf16[2048,256]{1,0:T(8,128)(2,1)S(1)} %get-tuple-element.26), kind=kLoop, calls=%fused_computation | loop fusion | flops 4194304 | bytes 4194304 | tf_op jit(solution)/shard_map/concatenate | solution.py:597
  93.7 0.0 collective-permute-done.3.refs_1_
  93.7 1.2 collective-permute-start.1
  94.9 0.0 collective-permute-done.4.refs_2_
  94.9 0.5 collective-permute-start
  95.4 0.0 collective-permute-done.5.refs_3_
  95.4 0.0 copy-done.9
  95.4 29.7 %shard_map.95 = (bf16[512,2048]{1,0:T(8,128)(2,1)}, bf16[2048,256]{1,0:T(8,128)(2,1)S(1)}, bf16[2048,256]{1,0:T(8,128)(2,1)S(1)}) custom-call(s32[3]{0:T(128)S(1)} %pad_add_fusion.1.base_ref, s32[8,8]{1,0:T(8,128)S(1)} %bitcast.5, s32[8]{0:T(128)S(1)} %bitcast.7, bf16[128,2048]{1,0:T(8,128)(2,1)S(1)} %copy-done.9, ...), custom_call_target="tpu_custom_call" | custom-call | flops 96636764160 | bytes 8388608 | tf_op jit(solution)/shard_map/pallas_call | solution.py:217
  125.1 0.0 collective-permute-done.2.r3
  125.1 0.0 collective-permute-done.1.r2
  125.1 0.0 collective-permute-done.r1
  125.1 0.0 collective-permute-done.7.y0
  125.1 0.0 copy-done
  125.1 56.9 %shard_map.96 = (bf16[128,8192]{1,0:T(8,128)(2,1)S(1)}, bf16[128,8192]{1,0:T(8,128)(2,1)S(1)}, bf16[128,1024]{1,0:T(8,128)(2,1)S(1)}, bf16[128,1024]{1,0:T(8,128)(2,1)S(1)}) custom-call(bf16[512,2048]{1,0:T(8,128)(2,1)S(1)} %copy-done, bf16[128,2048]{1,0:T(8,128)(2,1)S(1)} %collective-permute-done.r1, bf16[128,2048]{1,0:T(8,128)(2,1)S(1)} %collective-permute-done.1.r2, ...), custom_call_target="tpu_custom_call" | custom-call | tf_op jit(solution)/shard_map/pallas_call | solution.py:632
  182.1 1.3 copy.14
  183.4 1.3 copy.15
  184.7 0.7 copy.16
  185.4 0.7 copy.17
  (4 shorter events, 0.0 us)
Async XLA Ops:
  0.6 1.6 copy-start.1
  2.2 1.6 copy-start.2
  3.8 0.9 copy-start.3
  4.8 0.9 copy-start.4
  5.7 50.9 %copy-start.10 = (s32[1,8,8]{2,1,0:T(8,128)S(1)}, s32[1,8,8]{2,1,0:T(8,128)}, u32[]{:S(2)}) copy-start(s32[1,8,8]{2,1,0:T(8,128)} %param.10) | copy-start | bytes 772
  5.7 50.9 %copy-start.11 = (s32[1,8]{1,0:T(1,128)S(1)}, s32[1,8]{1,0:T(1,128)}, u32[]{:S(2)}) copy-start(s32[1,8]{1,0:T(1,128)} %param.11) | copy-start | bytes 100
  51.5 1.3 copy-start.5
  52.9 1.0 copy-start.6
  53.8 0.8 copy-start.8
  54.6 39.1 %collective-permute-start.3 = (bf16[128,2048]{1,0:T(8,128)(2,1)}, bf16[128,2048]{1,0:T(8,128)(2,1)}, u32[]{:S(2)}, u32[]{:S(2)}) collective-permute-start(bf16[128,2048]{1,0:T(8,128)(2,1)} %get-tuple-element.23), channel_id=1, source_target_pairs={{0,8},{8,16},{16,24},{24,0},{1,9},{9,17},{17,25},{25,1},{2,10},{10... | collective-permute-start | bytes 1572872 | tf_op jit(solution)/shard_map/ppermute | solution.py:553
  55.0 39.9 %collective-permute-start.4 = (bf16[128,2048]{1,0:T(8,128)(2,1)}, bf16[128,2048]{1,0:T(8,128)(2,1)}, u32[]{:S(2)}, u32[]{:S(2)}) collective-permute-start(bf16[128,2048]{1,0:T(8,128)(2,1)} %get-tuple-element.24), channel_id=1, source_target_pairs={{0,16},{8,24},{16,0},{24,8},{1,17},{9,25},{17,1},{25,9},{2,18},{10... | collective-permute-start | bytes 1572872 | tf_op jit(solution)/shard_map/ppermute | solution.py:553
  56.2 39.2 %collective-permute-start.5 = (bf16[128,2048]{1,0:T(8,128)(2,1)}, bf16[128,2048]{1,0:T(8,128)(2,1)}, u32[]{:S(2)}, u32[]{:S(2)}) collective-permute-start(bf16[128,2048]{1,0:T(8,128)(2,1)} %get-tuple-element.25), channel_id=1, source_target_pairs={{0,24},{8,0},{16,8},{24,16},{1,25},{9,1},{17,9},{25,17},{2,26},{10... | collective-permute-start | bytes 1572872 | tf_op jit(solution)/shard_map/ppermute | solution.py:553
  56.2 33.6 %collective-permute-start.6 = (bf16[2048,256]{1,0:T(8,128)(2,1)S(1)}, bf16[2048,256]{1,0:T(8,128)(2,1)}, u32[]{:S(2)}, u32[]{:S(2)}) collective-permute-start(bf16[2048,256]{1,0:T(8,128)(2,1)S(1)} %get-tuple-element.26), channel_id=1, source_target_pairs={{0,1},{1,0},{2,3},{3,2},{4,5},{5,4},{6,7},{7,6},{8,9},{9,8},{10,11... | collective-permute-start | bytes 3145736 | tf_op jit(solution)/shard_map/ppermute | solution.py:557
  56.6 1.2 copy-start.7
  87.1 38.0 %collective-permute-start.7 = (bf16[2048,256]{1,0:T(8,128)(2,1)}, bf16[2048,256]{1,0:T(8,128)(2,1)S(1)}, u32[]{:S(2)}, u32[]{:S(2)}) collective-permute-start(bf16[2048,256]{1,0:T(8,128)(2,1)} %get-tuple-element.29), channel_id=1, source_target_pairs={{0,1},{1,0},{2,3},{3,2},{4,5},{5,4},{6,7},{7,6},{8,9},{9,8},{10,11... | collective-permute-start | bytes 3145736 | tf_op jit(solution)/shard_map/ppermute | solution.py:557
  89.8 5.6 %copy-start.9 = (bf16[128,2048]{1,0:T(8,128)(2,1)S(1)}, bf16[128,2048]{1,0:T(8,128)(2,1)}, u32[]{:S(2)}) copy-start(bf16[128,2048]{1,0:T(8,128)(2,1)} %copy-done.8) | copy-start | bytes 1572868
  89.8 35.3 %collective-permute-start.2 = (bf16[128,2048]{1,0:T(8,128)(2,1)S(1)}, bf16[128,2048]{1,0:T(8,128)(2,1)S(1)}, u32[]{:S(2)}, u32[]{:S(2)}) collective-permute-start(bf16[128,2048]{1,0:T(8,128)(2,1)S(1)} %get-tuple-element.32), channel_id=1, source_target_pairs={{0,24},{8,0},{16,8},{24,16},{1,25},{9,1},{17,9},{25,17},{2,26},{10... | collective-permute-start | bytes 1572872 | tf_op jit(solution)/shard_map/ppermute | solution.py:553
  93.7 31.4 %collective-permute-start.1 = (bf16[128,2048]{1,0:T(8,128)(2,1)S(1)}, bf16[128,2048]{1,0:T(8,128)(2,1)S(1)}, u32[]{:S(2)}, u32[]{:S(2)}) collective-permute-start(bf16[128,2048]{1,0:T(8,128)(2,1)S(1)} %get-tuple-element.33), channel_id=1, source_target_pairs={{0,16},{8,24},{16,0},{24,8},{1,17},{9,25},{17,1},{25,9},{2,18},{10... | collective-permute-start | bytes 1572872 | tf_op jit(solution)/shard_map/ppermute | solution.py:553
  94.9 30.2 %collective-permute-start = (bf16[128,2048]{1,0:T(8,128)(2,1)S(1)}, bf16[128,2048]{1,0:T(8,128)(2,1)S(1)}, u32[]{:S(2)}, u32[]{:S(2)}) collective-permute-start(bf16[128,2048]{1,0:T(8,128)(2,1)S(1)} %get-tuple-element.34), channel_id=1, source_target_pairs={{0,8},{8,16},{16,24},{24,0},{1,9},{9,17},{17,25},{25,1},{2,10},{10... | collective-permute-start | bytes 1572872 | tf_op jit(solution)/shard_map/ppermute | solution.py:553
  95.4 29.7 %copy-start = (bf16[512,2048]{1,0:T(8,128)(2,1)S(1)}, bf16[512,2048]{1,0:T(8,128)(2,1)}, u32[]{:S(2)}) copy-start(bf16[512,2048]{1,0:T(8,128)(2,1)} %get-tuple-element.21.o0) | copy-start | bytes 6291460
